TPU v7x, 32 devices: a whole 2x2x4 slice. The times are simulated.
32 devices in a mesh: pool: 4 (over y, x), dev: 8 (over z, core).
Axes of the slice: x: 2, y: 2, z: 4, core: 2. Of those that a mesh axis runs over, the one named last changes fastest.
Arguments:
- patches: bfloat16 [64, 128, 1280], P('dev', 'pool'), may hold values from -6 to 6
- enc_tiles: int32 [8], replicated, may hold values from 1 to 8, 32 in all
- req_tiles: int32 [16], replicated, may hold values from 1 to 4, 32 in all
- req_owner: int32 [16, 1], replicated, may hold values from 0 to 3; in each aligned block of 16 rows (0 to 15, 16 to 31, ...) at most 6 rows name the same one
- fc1_weight: bfloat16 [1280, 5120], P(None, 'pool'), may hold values from -0.15625 to 0.15625
- fc2_weight: bfloat16 [5120, 1280], P('pool'), may hold values from -0.078125 to 0.078125
- key_weight: bfloat16 [1280, 1024], replicated, may hold values from -0.15625 to 0.15625
- value_weight: bfloat16 [1280, 1024], replicated, may hold values from -0.15625 to 0.15625
- query_weight: bfloat16 [8192, 8192], P(None, 'dev'), may hold values from -0.0625 to 0.0625
- out_weight: bfloat16 [8192, 8192], P('dev'), may hold values from -0.0625 to 0.0625
- text_hidden: bfloat16 [24, 4, 8192], P('pool'), may hold values from -6 to 6
Outputs:
- mixed: bfloat16 [24, 4, 8192], P('pool', None, 'dev')
Inputs may be any that keep to these rules, and one draw needn't show every extreme that they name: `enc_tiles`: the entries sum to 32; the largest is 8. `req_tiles`: the entries sum to 32; the largest is 4. `req_owner`: no group owns more than 6 requests, and some group owns exactly 6.
All inputs are finite; a program needn't handle non-finite values.
Results may differ from a plain program's by a relative error of at most 0.008.
Values may be sent and summed in bfloat16 or wider, within the bound.
A program may use at most 128 MiB of HBM per device.

v0:
```python
import jax
import jax.numpy as jnp
from jax import lax
from jax.sharding import PartitionSpec as P

HEADS = 64
KV_HEADS = 8
HEAD_DIM = 128
MAXT = 4


epsilon = 1e-05


def layer_stats(values_in):
    center = values_in - jnp.mean(values_in, axis=-1, keepdims=True)
    spread = jnp.mean(center * center, axis=-1, keepdims=True)
    return center / jnp.sqrt(spread + epsilon)


def rms_scale(values_in):
    return values_in / jnp.sqrt(jnp.mean(values_in * values_in, axis=-1, keepdims=True) + epsilon)


def slot_tables(enc_tiles, req_tiles, req_owner, groups, slots, capacity, most_tiles):
    enc_start = jnp.cumsum(enc_tiles) - enc_tiles
    req_start = jnp.cumsum(req_tiles) - req_tiles
    owner = req_owner[:, 0]
    group_ids = jnp.arange(groups, dtype=jnp.int32)
    member = (owner[:, None] == group_ids[None, :]).astype(jnp.int32)
    rank_in = jnp.sum((jnp.cumsum(member, axis=0) - 1) * member, axis=1)
    slot_ids = jnp.arange(slots, dtype=jnp.int32)
    match = (
        (owner[None, None, :] == group_ids[:, None, None])
        & (rank_in[None, None, :] == slot_ids[None, :, None])
    ).astype(jnp.int32)
    live = jnp.sum(match, axis=2) > 0
    length = jnp.sum(match * req_tiles[None, None, :], axis=2)
    first_tile = jnp.sum(match * req_start[None, None, :], axis=2)
    position = jnp.arange(most_tiles, dtype=jnp.int32)
    valid = position[None, None, :] < length[:, :, None]
    tile_index = first_tile[:, :, None] + position[None, None, :]
    column = jnp.sum((enc_start <= tile_index[..., None]).astype(jnp.int32), axis=-1) - 1
    column_hit = (column[..., None] == jnp.arange(enc_tiles.shape[0], dtype=jnp.int32)).astype(
        jnp.int32
    )
    column_start = jnp.sum(column_hit * enc_start, axis=-1)
    source = column * capacity + tile_index - column_start
    source = jnp.where(valid, source, 0)
    return (source, valid, live)


def place_tiles(received, source, valid):
    flat_rows = received.reshape((received.shape[0] * received.shape[1],) + received.shape[2:])
    picked = jnp.take(flat_rows, source.reshape(-1), axis=0)
    picked = picked.reshape(source.shape + flat_rows.shape[1:])
    return jnp.where(valid[..., None, None], picked, jnp.zeros_like(picked))


def body(
    patches,
    enc_tiles,
    req_tiles,
    req_owner,
    fc1_weight,
    fc2_weight,
    key_weight,
    value_weight,
    query_weight,
    out_weight,
    text_hidden,
):
    capacity, quarter, width_in = patches.shape
    groups = lax.axis_size("pool")
    devices = lax.axis_size("dev")
    share_count = devices // KV_HEADS
    local_heads = HEADS // devices
    slots, steps, model_width = text_hidden.shape
    flat_patches = patches.reshape(capacity * quarter, width_in)
    normed = layer_stats(flat_patches.astype(jnp.float32)).astype(jnp.bfloat16)
    widened = jax.nn.gelu(
        jnp.dot(
            lax.all_gather(normed, "pool", axis=0, tiled=True),
            fc1_weight,
            preferred_element_type=jnp.float32,
        ),
        approximate=False,
    ).astype(jnp.bfloat16)
    update = lax.psum_scatter(
        jnp.dot(widened, fc2_weight, preferred_element_type=jnp.float32),
        "pool",
        scatter_dimension=0,
        tiled=True,
    )
    vision = (flat_patches.astype(jnp.float32) + update).astype(jnp.bfloat16)
    key_rows = rms_scale(
        jnp.dot(vision, key_weight, preferred_element_type=jnp.float32).reshape(
            capacity * quarter, KV_HEADS, HEAD_DIM
        )
    ).astype(jnp.bfloat16)
    value_rows = (
        jnp.dot(vision, value_weight, preferred_element_type=jnp.float32)
        .astype(jnp.bfloat16)
        .reshape(capacity * quarter, KV_HEADS, HEAD_DIM)
    )
    paired_rows = jnp.concatenate([key_rows, value_rows], axis=-1).reshape(
        capacity, quarter, KV_HEADS, 2 * HEAD_DIM
    )
    heads_first = jnp.transpose(paired_rows, (2, 0, 1, 3))
    source, valid, live = slot_tables(
        enc_tiles, req_tiles, req_owner, groups, slots, capacity, MAXT
    )
    copies_out = jnp.repeat(heads_first, share_count, axis=0)
    received = lax.all_to_all(copies_out, "dev", split_axis=0, concat_axis=0, tiled=True)
    arrived = lax.all_to_all(
        place_tiles(received, source, valid), "pool", split_axis=0, concat_axis=0, tiled=True
    )
    group_index = lax.axis_index("pool")
    slot_valid = lax.dynamic_index_in_dim(valid, group_index, 0, keepdims=False).astype(jnp.float32)
    slot_live = lax.dynamic_index_in_dim(live, group_index, 0, keepdims=False)
    normed_text = (
        rms_scale(text_hidden.astype(jnp.float32))
        .astype(jnp.bfloat16)
        .reshape(slots * steps, model_width)
    )
    query = jnp.dot(normed_text, query_weight, preferred_element_type=jnp.float32).reshape(
        slots, steps * local_heads, HEAD_DIM
    )
    query = rms_scale(query).astype(jnp.bfloat16)
    scores = jnp.einsum(
        "rad,prmnd->rapmn", query, arrived[..., :HEAD_DIM], preferred_element_type=jnp.float32
    ) * HEAD_DIM ** (-0.5)
    weights = jnp.exp(scores) * slot_valid[:, None, None, :, None]
    total = jnp.sum(weights, axis=(2, 3, 4))
    total = jnp.where(slot_live[:, None], total, jnp.ones_like(total))
    weights = (weights / total[:, :, None, None, None]).astype(jnp.bfloat16)
    attended = jnp.einsum(
        "rapmn,prmnd->rad", weights, arrived[..., HEAD_DIM:], preferred_element_type=jnp.float32
    ).astype(jnp.bfloat16)
    partial_out = jnp.dot(
        attended.reshape(slots * steps, local_heads * HEAD_DIM),
        out_weight,
        preferred_element_type=jnp.float32,
    )
    summed = lax.psum_scatter(
        partial_out.astype(jnp.bfloat16), "dev", scatter_dimension=1, tiled=True
    ).astype(jnp.float32)
    width_out = model_width // devices
    residual = lax.dynamic_slice_in_dim(
        text_hidden, lax.axis_index("dev") * width_out, width_out, 2
    )
    mixed = (residual.reshape(slots * steps, width_out).astype(jnp.float32) + summed).astype(
        jnp.bfloat16
    )
    return mixed.reshape(slots, steps, width_out)


def solution(mesh):
    return jax.shard_map(
        body,
        mesh=mesh,
        in_specs=(
            P("dev", "pool", None),
            P(),
            P(),
            P(),
            P(None, "pool"),
            P("pool", None),
            P(),
            P(),
            P(None, "dev"),
            P("dev", None),
            P("pool", None, None),
        ),
        out_specs=P("pool", None, "dev"),
        check_vma=False,
    )
```

profile of v0, /device:TPU:0, one launch (start us, length us, event | category | flops | bytes accessed | tf_op | source)
XLA Modules:
  0.0 249.7 jit_solution(6541295207808753362)
XLA Ops:
  6.5 0.0 all-gather.2.cloned.1.call-start
  6.5 1.4 convert_reduce_fusion
  8.0 1.4 fusion.13
  9.4 0.1 div.72
  9.4 0.1 sqrt.41
  9.5 2.2 fusion.15
  11.7 0.0 all-gather.2.cloned.1.call-update
  11.7 0.0 reduce-scatter.3.cloned.1.call-start
  11.7 42.4 %all-gather.2.cloned.1.call-done = bf16[1024,1280]{1,0:T(8,128)(2,1)} async-done(((bf16[256,1280]{1,0:T(8,128)(2,1)}), bf16[1024,1280]{1,0:T(8,128)(2,1)}) %all-gather.2.cloned.1.call-update) | async-done | bytes 2621456 | tf_op jit(solution)/shard_map/all_gather | solution.py:83
  54.2 20.5 %fusion.10 = f32[1024,1280]{1,0:T(8,128)} fusion(bf16[1280,1280]{1,0:T(8,128)(2,1)S(1)} %copy-done, bf16[1024,1280]{1,0:T(8,128)(2,1)} %all-gather.2.cloned.1.call-done, bf16[1280,1280]{1,0:T(8,128)(2,1)} %param.15), kind=kOutput, calls=%fused_computation.21 | convolution fusion | flops 6796083200 | bytes 14417920 | tf_op jit(solution)/shard_map/dot_general | solution.py:90
  74.7 0.0 copy-start.3
  74.7 0.0 copy-start.2
  74.7 0.0 reduce-scatter.3.cloned.1.call-update
  74.8 0.6 copy-done.7
  75.4 0.1 copy.56
  75.4 0.1 fusion.29
  75.6 0.1 reduce.2
  75.7 0.2 select_reduce_fusion.1
  75.9 0.4 fusion.28
  76.3 0.1 copy.57
  76.4 0.2 reduce-window.18
  76.6 0.1 copy.55
  76.7 0.1 iota_add_fusion
  76.7 0.6 convert_reduce_fusion.1
  77.3 0.6 select_reduce_fusion
  77.9 0.1 compare_and_fusion
  78.0 0.1 reshape.358
  78.1 0.3 fusion.20
  78.4 58.0 %reduce-scatter.3.cloned.1.call-done = f32[256,1280]{1,0:T(8,128)} async-done(((f32[1024,1280]{1,0:T(8,128)}), f32[256,1280]{1,0:T(8,128)}) %reduce-scatter.3.cloned.1.call-update) | async-done | bytes 1310736 | tf_op jit(solution)/shard_map/reduce_scatter | solution.py:89
  136.4 1.4 fusion.16
  137.8 2.8 %fusion.65 = f32[256,1024]{1,0:T(8,128)S(1)} fusion(bf16[256,1280]{1,0:T(8,128)(2,1)S(1)} %fusion.16, bf16[1280,1024]{1,0:T(8,128)(2,1)} %param.17), kind=kOutput, calls=%fused_computation.120 | convolution fusion | flops 671088640 | bytes 4325376 | tf_op jit(solution)/shard_map/dot_general | solution.py:97
  140.7 0.1 multiply_bitcast_fusion
  140.8 0.2 copy.72
  141.0 0.3 reduce_sum.117
  141.4 0.1 copy.58
  141.5 0.2 copy.71
  141.7 0.0 copy-start.4
  141.7 2.8 %fusion.17 = bf16[32,8,8,128]{3,1,2,0:T(8,128)(2,1)S(1)} fusion(bf16[256,1280]{1,0:T(8,128)(2,1)} %copy-done.5, bf16[1280,1024]{1,0:T(8,128)(2,1)} %param.18), kind=kOutput, calls=%fused_computation.35 | convolution fusion | flops 671350784 | bytes 3801088 | tf_op jit(solution)/shard_map/dot_general | solution.py:102
  144.5 0.1 copy.73
  144.6 0.1 copy.60
  144.7 0.3 fusion.19
  145.1 1.2 maximum_bitcast_fusion
  146.2 4.6 %all-to-all-start = ((bf16[8,8,32,256]{3,2,1,0:T(8,128)(2,1)}), bf16[8,8,32,256]{3,2,1,0:T(8,128)(2,1)S(1)}, u32[]{:S(2)}, u32[]{:S(2)}) async-start(bf16[8,8,32,256]{3,2,1,0:T(8,128)(2,1)} %maximum_bitcast_fusion), calls=%async_computation.1 | async-start | bytes 2097152 | tf_op jit(solution)/shard_map/all_to_all | solution.py:114
  150.8 0.2 fusion.21
  151.1 0.1 reshape.345
  151.2 26.2 %all-to-all-done = bf16[8,8,32,256]{3,2,1,0:T(8,128)(2,1)S(1)} async-done(((bf16[8,8,32,256]{3,2,1,0:T(8,128)(2,1)}), bf16[8,8,32,256]{3,2,1,0:T(8,128)(2,1)S(1)}, u32[]{:S(2)}, u32[]{:S(2)}) %all-to-all-start) | async-done | bytes 1048608 | tf_op jit(solution)/shard_map/all_to_all | solution.py:114
  177.4 0.7 gather_fusion
  178.1 1.5 select_select_fusion
  179.6 3.6 %all-to-all-start.1 = ((bf16[4,6,4,32,256]{4,3,2,1,0:T(8,128)(2,1)}), bf16[4,6,4,32,256]{4,3,2,1,0:T(8,128)(2,1)S(1)}, u32[]{:S(2)}, u32[]{:S(2)}) async-start(bf16[4,6,4,32,256]{4,3,2,1,0:T(8,128)(2,1)} %select_select_fusion), calls=%async_computation.2 | async-start | bytes 3145728 | tf_op jit(solution)/shard_map/all_to_all | solution.py:115
  183.2 0.0 reduce-scatter.5.cloned.1.call-start
  183.2 8.0 %fusion.64 = f32[24,1024]{1,0:T(8,128)S(1)} fusion(bf16[24,8192]{1,0:T(8,128)(2,1)S(1)} %reshape.345, bf16[8192,1024]{1,0:T(8,128)(2,1)} %param.19), kind=kOutput, calls=%fused_computation.119 | convolution fusion | flops 402653184 | bytes 17268736 | tf_op jit(solution)/shard_map/dot_general | solution.py:126
  191.3 0.2 dynamic-slice_reduce_fusion
  191.5 0.1 multiply_reduce_fusion
  191.6 10.8 %all-to-all-done.1 = bf16[4,6,4,32,256]{4,3,2,1,0:T(8,128)(2,1)S(1)} async-done(((bf16[4,6,4,32,256]{4,3,2,1,0:T(8,128)(2,1)}), bf16[4,6,4,32,256]{4,3,2,1,0:T(8,128)(2,1)S(1)}, u32[]{:S(2)}, u32[]{:S(2)}) %all-to-all-start.1) | async-done | bytes 1572896 | tf_op jit(solution)/shard_map/all_to_all | solution.py:115
  202.5 0.6 fusion.61
  203.0 0.1 broadcast_select_fusion
  203.1 0.4 fusion.18
  203.5 0.0 copy-start.1
  203.6 9.0 %convolution_convert_fusion = bf16[24,8192]{1,0:T(8,128)(2,1)} fusion(bf16[24,1024]{1,0:T(8,128)(2,1)S(1)} %reshape.353, bf16[1024,8192]{1,0:T(8,128)(2,1)} %param.20), kind=kOutput, calls=%fused_computation.1 | convolution fusion | flops 402849792 | bytes 17219584 | tf_op jit(solution)/shard_map/dot_general | solution.py:140
  212.5 0.0 reduce-scatter.5.cloned.1.call-update
  212.5 0.8 dynamic-slice_convert_fusion
  213.4 28.3 %reduce-scatter.5.cloned.1.call-done = bf16[24,1024]{1,0:T(8,128)(2,1)} async-done(((bf16[24,8192]{1,0:T(8,128)(2,1)}), bf16[24,1024]{1,0:T(8,128)(2,1)}) %reduce-scatter.5.cloned.1.call-update) | async-done | bytes 49168 | tf_op jit(solution)/shard_map/reduce_scatter | solution.py:145
  241.7 0.8 add_convert_fusion
  242.5 0.6 reshape.354
  (32 shorter events, 0.3 us)
Async XLA Ops:
  6.5 47.7 %copy-start = (bf16[1280,1280]{1,0:T(8,128)(2,1)S(1)}, bf16[1280,1280]{1,0:T(8,128)(2,1)}, u32[]{:S(2)}) copy-start(bf16[1280,1280]{1,0:T(8,128)(2,1)} %param.16) | copy-start | bytes 9830404
  6.5 47.7 %all-gather.2.cloned.1.call-start = ((), (), s32[]{:S(2)}) async-start(), calls=%async_computation.4 | async-start | bytes 3276800 | tf_op jit(solution)/shard_map/all_gather | solution.py:83
  11.7 124.7 %reduce-scatter.3.cloned.1.call-start = ((), (), s32[]{:S(2)}) async-start(), calls=%async_computation.5 | async-start | bytes 6553600 | tf_op jit(solution)/shard_map/reduce_scatter | solution.py:89
  74.7 0.7 copy-start.7
  74.7 0.7 copy-start.6
  74.7 1.7 copy-start.8
  74.7 3.4 %copy-start.3 = (bf16[6,4,8192]{2,1,0:T(4,128)(2,1)S(1)}, bf16[6,4,8192]{2,1,0:T(4,128)(2,1)}, u32[]{:S(2)}) copy-start(bf16[6,4,8192]{2,1,0:T(4,128)(2,1)} %param.21) | copy-start | bytes 1179652
  74.7 61.7 %copy-start.2 = (bf16[8,32,1280]{2,1,0:T(8,128)(2,1)S(1)}, bf16[8,32,1280]{2,1,0:T(8,128)(2,1)}, u32[]{:S(2)}) copy-start(bf16[8,32,1280]{2,1,0:T(8,128)(2,1)} %param.11) | copy-start | bytes 1966084
  137.8 2.8 %copy-start.5 = (bf16[256,1280]{1,0:T(8,128)(2,1)}, bf16[256,1280]{1,0:T(8,128)(2,1)S(1)}, u32[]{:S(2)}) copy-start(bf16[256,1280]{1,0:T(8,128)(2,1)S(1)} %fusion.16) | copy-start | bytes 1966084
  141.7 9.2 %copy-start.4 = (bf16[6,4,8192]{2,1,0:T(4,128)(2,1)S(1)}, bf16[6,4,8192]{2,1,0:T(4,128)(2,1)}, u32[]{:S(2)}) copy-start(bf16[6,4,8192]{2,1,0:T(4,128)(2,1)} %param.21) | copy-start | bytes 1179652
  146.2 31.2 %all-to-all-start = ((bf16[8,8,32,256]{3,2,1,0:T(8,128)(2,1)}), bf16[8,8,32,256]{3,2,1,0:T(8,128)(2,1)S(1)}, u32[]{:S(2)}, u32[]{:S(2)}) async-start(bf16[8,8,32,256]{3,2,1,0:T(8,128)(2,1)} %maximum_bitcast_fusion), calls=%async_computation.1 | async-start | bytes 2097152 | tf_op jit(solution)/shard_map/all_to_all | solution.py:114
  179.6 22.9 %all-to-all-start.1 = ((bf16[4,6,4,32,256]{4,3,2,1,0:T(8,128)(2,1)}), bf16[4,6,4,32,256]{4,3,2,1,0:T(8,128)(2,1)S(1)}, u32[]{:S(2)}, u32[]{:S(2)}) async-start(bf16[4,6,4,32,256]{4,3,2,1,0:T(8,128)(2,1)} %select_select_fusion), calls=%async_computation.2 | async-start | bytes 3145728 | tf_op jit(solution)/shard_map/all_to_all | solution.py:115
  183.2 58.5 %reduce-scatter.5.cloned.1.call-start = ((), (), s32[]{:S(2)}) async-start(), calls=%async_computation.6 | async-start | bytes 442368 | tf_op jit(solution)/shard_map/reduce_scatter | solution.py:145
  203.5 39.6 %copy-start.1 = (bf16[1280,1280]{1,0:T(8,128)(2,1)S(1)}, bf16[1280,1280]{1,0:T(8,128)(2,1)}, u32[]{:S(2)}) copy-start(bf16[1280,1280]{1,0:T(8,128)(2,1)} %param.16) | copy-start | bytes 9830404
Sparse Core Ops, SparseCore 0:
  11.8 42.3 all-gather.1
  74.9 61.4 reduce-scatter.2
  212.7 28.9 reduce-scatter.4
where the time goes:
time: 250 us
  waiting for transfers between devices  166 us (66%)
  matrix products  44.1 us (18%)
  other arithmetic  14.5 us (6%)
  between operations  13.4 us (5%)
  starting transfers between devices  8.23 us (3%)
  local copies, waits for them, and re-layouts  3.57 us (1%)
    reduce_scatter x1, waiting for transfers between devices, body(): lax.psum_scatter(jnp.dot(widened, fc2_weight, preferred_element_type=jnp....  58 us
    all_gather x1, waiting for transfers between devices, body(): lax.all_gather(normed, 'pool', axis=0, tiled=True)  42.4 us
    reduce_scatter x1, waiting for transfers between devices, body(): lax.psum_scatter(partial_out.astype(jnp.bfloat16), 'dev', scatter_dimensi...  28.3 us
    all_to_all x1, waiting for transfers between devices, body(): lax.all_to_all(copies_out, 'dev', split_axis=0, concat_axis=0, tiled=True)  26.2 us
    dot_general x1, matrix products, body(): jnp.dot(widened, fc2_weight, preferred_element_type=jnp.float32)  20.5 us
    all_to_all x1, waiting for transfers between devices, body(): lax.all_to_all(place_tiles(received, source, valid), 'pool', split_axis=0...  10.8 us
    dot_general x1, matrix products, body(): jnp.dot(attended.reshape(slots * steps, local_heads * HEAD_DIM), out_weig...  8.96 us
    dot_general x1, matrix products, body(): jnp.dot(normed_text, query_weight, preferred_element_type=jnp.float32)  8.04 us
  transfers between devices with their start and end apart: 5, of which 5 were waited for; matrix products, arithmetic and copies ran while one was open for 5% of the time, Pallas kernels for 0%

commit v1 on v0

--- a/solution.py
+++ b/solution.py
@@ -1,7 +1,11 @@
 import jax
 import jax.numpy as jnp
 from jax import lax
+from jax.experimental import pallas as pl
+from jax.experimental.pallas import tpu as pltpu
 from jax.sharding import PartitionSpec as P
+
+MESH = pl.DeviceIdType.MESH
 
 HEADS = 64
 KV_HEADS = 8
@@ -155,9 +159,523 @@
     return mixed.reshape(slots, steps, width_out)
 
 
+def remote(source, target, send_sems, recv_sems, index, device):
+    return pltpu.make_async_remote_copy(
+        src_ref=source,
+        dst_ref=target,
+        send_sem=send_sems.at[index],
+        recv_sem=recv_sems.at[index],
+        device_id=device,
+        device_id_type=MESH,
+    )
+
+
+def greet(pool_peers, dev_peers):
+    barrier = pltpu.get_barrier_semaphore()
+    for peer in pool_peers + dev_peers:
+        pl.semaphore_signal(barrier, inc=1, device_id=peer, device_id_type=MESH)
+    pl.semaphore_wait(barrier, len(pool_peers) + len(dev_peers))
+
+
+def vision_kernel(
+    patches_ref,
+    text_ref,
+    fc1_hbm,
+    fc2_hbm,
+    key_hbm,
+    value_hbm,
+    query_hbm,
+    kv_out,
+    query_out,
+    fc1,
+    fc2,
+    key_map,
+    value_map,
+    query_map,
+    rows,
+    hidden,
+    partial,
+    own_sum,
+    late_sum,
+    outbox,
+    diagonal_in,
+    x_in,
+    y_in,
+    kv_box,
+    kv_all,
+    text_normed,
+    query_sum,
+    query_flat,
+    query_all,
+    local_sems,
+    send_sems,
+    recv_sems,
+):
+    pool, dev = lax.axis_index("pool"), lax.axis_index("dev")
+    x, y = lax.rem(pool, 2), lax.div(pool, 2)
+    x_peer = (y * 2 + 1 - x, dev)
+    y_peer = ((1 - y) * 2 + x, dev)
+    devices = kv_all.shape[0]
+    chunks = rows.shape[0]
+    part = rows.shape[1] // 4
+    width = rows.shape[2]
+    tile = 256
+
+    loads = [
+        pltpu.make_async_copy(fc1_hbm, fc1, local_sems.at[0]),
+        pltpu.make_async_copy(fc2_hbm, fc2, local_sems.at[1]),
+        pltpu.make_async_copy(key_hbm, key_map, local_sems.at[2]),
+        pltpu.make_async_copy(value_hbm, value_map, local_sems.at[3]),
+    ]
+    pieces = query_map.shape[0]
+    depth = query_map.shape[1]
+    query_loads = [
+        pltpu.make_async_copy(
+            query_hbm.at[pl.ds(k * depth, depth), :], query_map.at[k], local_sems.at[4 + k]
+        )
+        for k in range(pieces)
+    ]
+    loads[0].start()
+    loads[1].start()
+    for load in query_loads:
+        load.start()
+    loads[2].start()
+    loads[3].start()
+
+    pool_peers = [(lax.rem(pool + k, 4), dev) for k in range(1, 4)]
+    dev_peers = [(pool, lax.rem(dev + k, devices)) for k in range(1, devices)]
+    greet(pool_peers, dev_peers)
+
+    count = [0]
+
+    def send(source, target, device):
+        copy = remote(source, target, send_sems, recv_sems, count[0], device)
+        count[0] += 1
+        return copy
+
+    def block(c, k):
+        return rows.at[c, pl.ds(k * part, part)]
+
+    to_x = [send(block(c, 0), block(c, 1), x_peer) for c in range(chunks)]
+    to_y = [send(block(c, 0), block(c, 2), y_peer) for c in range(chunks)]
+    half = chunks // 2
+    onward = [
+        send(block(c, 1), block(c, 3), y_peer)
+        if c < half
+        else send(block(c, 2), block(c, 3), x_peer)
+        for c in range(chunks)
+    ]
+
+    def normalize(c):
+        values = patches_ref[c * part : (c + 1) * part, :].astype(jnp.float32)
+        rows[c, 0:part, :] = layer_stats(values).astype(jnp.bfloat16)
+
+    for c in range(chunks):
+        normalize(c)
+        if c < half:
+            to_x[c].start()
+            to_y[c].start()
+
+    text_normed[...] = rms_scale(text_ref[...].astype(jnp.float32))
+    query_sum[...] = jnp.zeros_like(query_sum)
+
+    def query_step(k):
+        query_loads[k].wait()
+        query_sum[...] += jnp.dot(
+            text_normed[:, k * depth : (k + 1) * depth].astype(jnp.bfloat16),
+            query_map[k],
+            preferred_element_type=jnp.float32,
+        )
+
+    for c in range(half):
+        query_step(2 * c)
+        query_step(2 * c + 1)
+        to_x[c].wait_recv()
+        onward[c].start()
+        to_x[half + c].start()
+        to_y[half + c].start()
+    for k in range(2 * half, pieces):
+        query_step(k)
+    text_rows = query_sum.shape[0]
+    for h in range(query_sum.shape[1] // HEAD_DIM):
+        query_flat[h * text_rows : (h + 1) * text_rows, :] = rms_scale(
+            query_sum[:, h * HEAD_DIM : (h + 1) * HEAD_DIM]
+        )
+    query_all[pool] = query_flat[...].astype(jnp.bfloat16)
+    query_sends = [send(query_all.at[pool], query_all.at[pool], peer) for peer in pool_peers]
+    for copy in query_sends:
+        copy.start()
+
+    def feed_forward(c):
+        def widen(n, carry):
+            columns = pl.ds(pl.multiple_of(n * tile, tile), tile)
+            pre = jnp.dot(rows[c], fc1[:, columns], preferred_element_type=jnp.float32)
+            hidden[:, columns] = (0.5 * pre * (1.0 + lax.erf(pre * 0.7071067811865476))).astype(
+                jnp.bfloat16
+            )
+            return carry
+
+        def narrow(n, carry):
+            columns = pl.ds(pl.multiple_of(n * tile, tile), tile)
+            partial[:, columns] = jnp.dot(
+                hidden[...], fc2[:, columns], preferred_element_type=jnp.float32
+            )
+            return carry
+
+        lax.fori_loop(0, fc1.shape[1] // tile, widen, 0)
+        lax.fori_loop(0, width // tile, narrow, 0)
+        own_sum[c] = partial[0:part, :]
+        late = 2 if c < half else 1
+        late_sum[c] = partial[late * part : (late + 1) * part, :]
+        early = 3 - late
+        outbox[c, 0] = partial[3 * part : 4 * part, :].astype(jnp.bfloat16)
+        outbox[c, 1] = partial[early * part : (early + 1) * part, :].astype(jnp.bfloat16)
+        peer = x_peer if c < half else y_peer
+        arrival = x_in if c < half else y_in
+        copies = [
+            send(outbox.at[c, 0], diagonal_in.at[c], peer),
+            send(outbox.at[c, 1], arrival.at[c], peer),
+        ]
+        for copy in copies:
+            copy.start()
+        return copies
+
+    def pass_on(c, copies):
+        copies[0].wait_recv()
+        outbox[c, 2] = (late_sum[c] + diagonal_in[c].astype(jnp.float32)).astype(jnp.bfloat16)
+        peer = y_peer if c < half else x_peer
+        arrival = y_in if c < half else x_in
+        copy = send(outbox.at[c, 2], arrival.at[c], peer)
+        copy.start()
+        copies.append(copy)
+
+    def project(c, copies):
+        copies[1].wait_recv()
+        copies[2].wait_recv()
+        if c == 0:
+            loads[2].wait()
+            loads[3].wait()
+        update = own_sum[c] + x_in[c].astype(jnp.float32) + y_in[c].astype(jnp.float32)
+        vision = (
+            patches_ref[c * part : (c + 1) * part, :].astype(jnp.float32) + update
+        ).astype(jnp.bfloat16)
+        pair = 2 * HEAD_DIM
+
+        def two_heads(n, carry):
+            columns = pl.ds(pl.multiple_of(n * pair, pair), pair)
+            keys = jnp.dot(vision, key_map[:, columns], preferred_element_type=jnp.float32)
+            values = jnp.dot(vision, value_map[:, columns], preferred_element_type=jnp.float32)
+            for i in range(2):
+                lanes = slice(i * HEAD_DIM, (i + 1) * HEAD_DIM)
+                kv_box[c, 2 * n + i, :, 0:HEAD_DIM] = rms_scale(keys[:, lanes]).astype(jnp.bfloat16)
+                kv_box[c, 2 * n + i, :, HEAD_DIM:pair] = values[:, lanes].astype(jnp.bfloat16)
+            return carry
+
+        lax.fori_loop(0, KV_HEADS // 2, two_heads, 0)
+        kv_all[dev, c] = kv_box[c, dev]
+        for peer in dev_peers:
+            copy = send(kv_box.at[c, peer[1]], kv_all.at[dev, c], peer)
+            copy.start()
+            kv_sends.append(copy)
+
+    kv_sends = []
+    sums = [None] * chunks
+    for c in range(half):
+        to_y[c].wait_recv()
+        onward[c].wait_recv()
+        if c == 0:
+            loads[0].wait()
+            loads[1].wait()
+        sums[c] = feed_forward(c)
+        to_y[half + c].wait_recv()
+        onward[half + c].start()
+    pass_on(0, sums[0])
+    for c in range(half, chunks):
+        to_x[c].wait_recv()
+        onward[c].wait_recv()
+        sums[c] = feed_forward(c)
+        pass_on(c - half + 1, sums[c - half + 1])
+        project(c - half, sums[c - half])
+    for c in range(half + 1, chunks):
+        pass_on(c, sums[c])
+    for c in range(half, chunks):
+        project(c, sums[c])
+
+    for copy in query_sends:
+        copy.wait_recv()
+    query_out[...] = query_all[...]
+    for copy in kv_sends:
+        copy.wait_recv()
+    kv_out[...] = kv_all[...]
+    for copy in to_x + to_y + onward + query_sends + kv_sends:
+        copy.wait_send()
+    for copies in sums:
+        for copy in copies:
+            copy.wait_send()
+
+
+def decode_kernel(
+    query_ref,
+    kv_ref,
+    member_ref,
+    text_ref,
+    out_hbm,
+    mixed_ref,
+    out_map,
+    mask,
+    gathered,
+    outbox,
+    inbox,
+    attended,
+    piece_out,
+    piece_in,
+    local_sems,
+    send_sems,
+    recv_sems,
+):
+    pool, dev = lax.axis_index("pool"), lax.axis_index("dev")
+    devices = out_map.shape[0]
+    width_out = out_map.shape[2]
+    text_rows = text_ref.shape[0]
+    order = list(range(1, devices)) + [0]
+    loads = []
+    for k in order:
+        start = pl.multiple_of(lax.rem(dev + k, devices) * width_out, width_out)
+        load = pltpu.make_async_copy(
+            out_hbm.at[:, pl.ds(start, width_out)], out_map.at[k], local_sems.at[k]
+        )
+        load.start()
+        loads.append(load)
+    pool_peers = [(lax.rem(pool + k, 4), dev) for k in range(1, 4)]
+    dev_peers = [(pool, lax.rem(dev + k, devices)) for k in range(1, devices)]
+    greet(pool_peers, dev_peers)
+
+    slots_all, keys_all = member_ref.shape[1], kv_ref.shape[0]
+    quarter = keys_all // slots_all
+    first = lax.broadcasted_iota(jnp.int32, (slots_all, keys_all), 0) * quarter
+    column = lax.broadcasted_iota(jnp.int32, (slots_all, keys_all), 1)
+    spread = jnp.where((column >= first) & (column < first + quarter), 1.0, 0.0).astype(
+        jnp.bfloat16
+    )
+    for g in range(4):
+        mask[g] = jnp.dot(
+            member_ref[g * text_rows : (g + 1) * text_rows, :].astype(jnp.bfloat16),
+            spread,
+            preferred_element_type=jnp.float32,
+        )
+
+    span = 512
+    heads = query_ref.shape[1] // text_rows
+
+    def attend(group):
+        gathered[...] = jnp.zeros_like(gathered)
+
+        def step(b, carry):
+            rows = pl.ds(pl.multiple_of(b * span, span), span)
+            scores = lax.dot_general(
+                query_ref[group],
+                kv_ref[rows, 0:HEAD_DIM],
+                (((1,), (1,)), ((), ())),
+                preferred_element_type=jnp.float32,
+            ) * HEAD_DIM ** (-0.5)
+            weights = jnp.exp(scores).reshape(heads, text_rows, span) * mask[group, :, rows][None]
+            values = jnp.concatenate(
+                [kv_ref[rows, HEAD_DIM : 2 * HEAD_DIM], jnp.ones((span, HEAD_DIM), jnp.bfloat16)],
+                axis=1,
+            )
+            gathered[...] += jnp.dot(
+                weights.reshape(heads * text_rows, span).astype(jnp.bfloat16),
+                values,
+                preferred_element_type=jnp.float32,
+            )
+            return carry
+
+        lax.fori_loop(0, keys_all // span, step, 0)
+
+    lane = lax.broadcasted_iota(jnp.int32, (heads * text_rows, HEAD_DIM), 1)
+    sends = []
+    for k, peer in enumerate(pool_peers):
+        attend(peer[0])
+        total = gathered[:, HEAD_DIM : 2 * HEAD_DIM]
+        coarse = total.astype(jnp.bfloat16).astype(jnp.float32)
+        outbox[k, :, 0:HEAD_DIM] = gathered[:, 0:HEAD_DIM].astype(jnp.bfloat16)
+        outbox[k, :, HEAD_DIM : 2 * HEAD_DIM] = jnp.where(
+            lane < HEAD_DIM // 2, coarse, total - coarse
+        ).astype(jnp.bfloat16)
+        copy = remote(outbox.at[k], inbox.at[k], send_sems, recv_sems, k, peer)
+        copy.start()
+        sends.append(copy)
+    attend(pool)
+    for k, copy in enumerate(sends):
+        copy.wait_recv()
+        arrived = inbox[k].astype(jnp.float32)
+        total = (
+            arrived[:, HEAD_DIM : HEAD_DIM + 1]
+            + arrived[:, HEAD_DIM + HEAD_DIM // 2 : HEAD_DIM + HEAD_DIM // 2 + 1]
+        )
+        gathered[:, 0:HEAD_DIM] += arrived[:, 0:HEAD_DIM]
+        gathered[:, HEAD_DIM : 2 * HEAD_DIM] += jnp.broadcast_to(total, (total.shape[0], HEAD_DIM))
+    total = gathered[:, HEAD_DIM : 2 * HEAD_DIM]
+    result = gathered[:, 0:HEAD_DIM] / jnp.where(total > 0.0, total, 1.0)
+    for h in range(heads):
+        attended[:, h * HEAD_DIM : (h + 1) * HEAD_DIM] = result[
+            h * text_rows : (h + 1) * text_rows, :
+        ]
+    left = attended[...].astype(jnp.bfloat16)
+    half = width_out // 2
+    copies = []
+    for i, k in enumerate(order):
+        loads[i].wait()
+        product = jnp.dot(left, out_map[k], preferred_element_type=jnp.float32)
+        if k > 0:
+            piece_out[k - 1] = jnp.concatenate([product[:, :half], product[:, half:]], axis=0).astype(
+                jnp.bfloat16
+            )
+            copy = remote(
+                piece_out.at[k - 1], piece_in.at[k - 1], send_sems, recv_sems, 2 + k, dev_peers[k - 1]
+            )
+            copy.start()
+            copies.append(copy)
+    folded = jnp.concatenate([product[:, :half], product[:, half:]], axis=0)
+    for k, copy in enumerate(copies):
+        copy.wait_recv()
+        folded = folded + piece_in[k].astype(jnp.float32)
+    own = pl.ds(pl.multiple_of(dev * width_out, width_out), width_out)
+    residual = text_ref[:, own].astype(jnp.float32)
+    summed = jnp.concatenate([folded[:text_rows], folded[text_rows:]], axis=1)
+    mixed_ref[...] = (residual + summed).astype(jnp.bfloat16)
+    for copy in sends + copies:
+        copy.wait_send()
+
+
+def membership(enc_tiles, req_tiles, req_owner, groups, slots, steps, capacity):
+    requests = req_tiles.shape[0]
+    enc_start = jnp.cumsum(enc_tiles) - enc_tiles
+    req_start = jnp.cumsum(req_tiles) - req_tiles
+    owner = req_owner[:, 0]
+    order = jnp.arange(requests, dtype=jnp.int32)
+    earlier = (owner[:, None] == owner[None, :]) & (order[None, :] < order[:, None])
+    rank = jnp.sum(earlier.astype(jnp.int32), axis=1)
+    place = jnp.arange(capacity, dtype=jnp.int32)
+    tile = (enc_start[:, None] + place[None, :]).reshape(-1)
+    tile_live = (place[None, :] < enc_tiles[:, None]).reshape(-1)
+    holds = (
+        tile_live[None, :]
+        & (tile[None, :] >= req_start[:, None])
+        & (tile[None, :] < (req_start + req_tiles)[:, None])
+    )
+    slot = jnp.arange(groups * slots * steps, dtype=jnp.int32) // steps
+    mine = slot[:, None] == (owner * slots + rank)[None, :]
+    return jnp.any(mine[:, :, None] & holds[None, :, :], axis=1).astype(jnp.float32)
+
+
+def fused_body(
+    patches,
+    enc_tiles,
+    req_tiles,
+    req_owner,
+    fc1_weight,
+    fc2_weight,
+    key_weight,
+    value_weight,
+    query_weight,
+    out_weight,
+    text_hidden,
+):
+    capacity, quarter, width = patches.shape
+    slots, steps, model_width = text_hidden.shape
+    groups, devices = lax.axis_size("pool"), lax.axis_size("dev")
+    local = query_weight.shape[1]
+    heads = local // HEAD_DIM
+    chunks = 4
+    count = capacity * quarter
+    part = count // chunks
+    text_rows = slots * steps
+    text = text_hidden.reshape(text_rows, model_width)
+    vmem = pl.BlockSpec(memory_space=pltpu.VMEM)
+    anywhere = pl.BlockSpec(memory_space=pl.ANY)
+    bf16, f32 = jnp.bfloat16, jnp.float32
+    pieces = 8
+    copies = 6 * chunks + (groups - 1) + chunks * (devices - 1)
+    kv, queries = pl.pallas_call(
+        vision_kernel,
+        out_shape=(
+            jax.ShapeDtypeStruct((devices, chunks, part, 2 * HEAD_DIM), bf16),
+            jax.ShapeDtypeStruct((groups, heads * text_rows, HEAD_DIM), bf16),
+        ),
+        in_specs=[vmem, vmem] + [anywhere] * 5,
+        out_specs=(vmem, vmem),
+        scratch_shapes=[
+            pltpu.VMEM(fc1_weight.shape, bf16),
+            pltpu.VMEM(fc2_weight.shape, bf16),
+            pltpu.VMEM(key_weight.shape, bf16),
+            pltpu.VMEM(value_weight.shape, bf16),
+            pltpu.VMEM((pieces, model_width // pieces, local), bf16),
+            pltpu.VMEM((chunks, 4 * part, width), bf16),
+            pltpu.VMEM((4 * part, fc1_weight.shape[1]), bf16),
+            pltpu.VMEM((4 * part, width), f32),
+            pltpu.VMEM((chunks, part, width), f32),
+            pltpu.VMEM((chunks, part, width), f32),
+            pltpu.VMEM((chunks, 3, part, width), bf16),
+            pltpu.VMEM((chunks, part, width), bf16),
+            pltpu.VMEM((chunks, part, width), bf16),
+            pltpu.VMEM((chunks, part, width), bf16),
+            pltpu.VMEM((chunks, KV_HEADS, part, 2 * HEAD_DIM), bf16),
+            pltpu.VMEM((devices, chunks, part, 2 * HEAD_DIM), bf16),
+            pltpu.VMEM((text_rows, model_width), f32),
+            pltpu.VMEM((text_rows, local), f32),
+            pltpu.VMEM((heads * text_rows, HEAD_DIM), f32),
+            pltpu.VMEM((groups, heads * text_rows, HEAD_DIM), bf16),
+            pltpu.SemaphoreType.DMA((4 + pieces,)),
+            pltpu.SemaphoreType.DMA((copies,)),
+            pltpu.SemaphoreType.DMA((copies,)),
+        ],
+        compiler_params=pltpu.CompilerParams(
+            collective_id=0, has_side_effects=True, vmem_limit_bytes=56 * 1024 * 1024
+        ),
+        name="vision",
+    )(
+        patches.reshape(count, width),
+        text,
+        fc1_weight,
+        fc2_weight,
+        key_weight,
+        value_weight,
+        query_weight,
+    )
+    member = membership(enc_tiles, req_tiles, req_owner, groups, slots, steps, capacity)
+    width_out = model_width // devices
+    piece = (devices - 1, 2 * text_rows, width_out // 2)
+    mixed = pl.pallas_call(
+        decode_kernel,
+        out_shape=jax.ShapeDtypeStruct((text_rows, width_out), bf16),
+        in_specs=[vmem] * 4 + [anywhere],
+        out_specs=vmem,
+        scratch_shapes=[
+            pltpu.VMEM((devices, local, width_out), bf16),
+            pltpu.VMEM((groups, text_rows, devices * count), f32),
+            pltpu.VMEM((heads * text_rows, 2 * HEAD_DIM), f32),
+            pltpu.VMEM((groups - 1, heads * text_rows, 2 * HEAD_DIM), bf16),
+            pltpu.VMEM((groups - 1, heads * text_rows, 2 * HEAD_DIM), bf16),
+            pltpu.VMEM((text_rows, local), f32),
+            pltpu.VMEM(piece, bf16),
+            pltpu.VMEM(piece, bf16),
+            pltpu.SemaphoreType.DMA((devices,)),
+            pltpu.SemaphoreType.DMA((devices + groups,)),
+            pltpu.SemaphoreType.DMA((devices + groups,)),
+        ],
+        compiler_params=pltpu.CompilerParams(
+            collective_id=1, has_side_effects=True, vmem_limit_bytes=48 * 1024 * 1024
+        ),
+        name="decode",
+    )(queries, kv.reshape(devices * count, 2 * HEAD_DIM), member, text, out_weight)
+    return mixed.reshape(slots, steps, width_out)
+
+
 def solution(mesh):
+    fits = mesh.shape["pool"] == 4 and mesh.shape["dev"] == KV_HEADS
     return jax.shard_map(
-        body,
+        fused_body if fits else body,
         mesh=mesh,
         in_specs=(
             P("dev", "pool", None),

time: 250 us -> 104 us (0.42)
  waiting for transfers between devices: 166 us -> 0 us
  Pallas kernels: 0 us -> 92.1 us
  matrix products: 44.1 us -> 0 us
  between operations: 13.4 us -> 0.06 us
  other arithmetic: 14.5 us -> 5.04 us
  starting transfers between devices: 8.23 us -> 0 us
    pallas_call x0 -> x2, Pallas kernels: none -> 92.1 us  [the longest x1 70.5 us: fused_body(): pl.pallas_call(vision_kernel, out_shape=(jax.ShapeDtypeStruct((devices, c...]
    reduce_scatter x2 -> x0, waiting for transfers between devices: 86.3 us -> none  [the longest x1 58 us: body(): lax.psum_scatter(jnp.dot(widened, fc2_weight, preferred_element_type=jnp....]
    dot_general x7 -> x0, matrix products: 44.1 us -> none  [the longest x1 20.5 us: body(): jnp.dot(widened, fc2_weight, preferred_element_type=jnp.float32)]
    all_gather x1 -> x0, waiting for transfers between devices: 42.4 us -> none  [body(): lax.all_gather(normed, 'pool', axis=0, tiled=True)]
    all_to_all x2 -> x0, waiting for transfers between devices: 37.1 us -> none  [the longest x1 26.2 us: body(): lax.all_to_all(copies_out, 'dev', split_axis=0, concat_axis=0, tiled=True)]
    all_to_all x2 -> x0, starting transfers between devices: 8.15 us -> none  [the longest x1 4.59 us: body(): lax.all_to_all(copies_out, 'dev', split_axis=0, concat_axis=0, tiled=True)]
    convert_element_type x8 -> x1, other arithmetic: 5.84 us -> 0.01 us  [membership(): jnp.any(mine[:, :, None] & holds[None, :, :], axis=1).astype(jnp.float32)]
    reduce_sum x9 -> x1, other arithmetic: 5.21 us -> 0.91 us  [membership(): rank = jnp.sum(earlier.astype(jnp.int32), axis=1)]
  transfers between devices with their start and end apart: 5 -> 0, of which waited for: 5 -> 0; matrix products, arithmetic and copies ran while one was open for 5% -> 0% of each run, Pallas kernels for 0% -> 0%
where the time goes in v1:
time: 104 us; the launch traced here: 103 us
  Pallas kernels  92.1 us (89%)
  local copies, waits for them, and re-layouts  5.62 us (5%)
  other arithmetic  5.04 us (5%)
    pallas_call x1, Pallas kernels, fused_body(): pl.pallas_call(vision_kernel, out_shape=(jax.ShapeDtypeStruct((devices, c...  70.5 us
    pallas_call x1, Pallas kernels, fused_body(): pl.pallas_call(decode_kernel, out_shape=jax.ShapeDtypeStruct((text_rows,...  21.6 us
    unnamed x6, local copies, waits for them, and re-layouts  2.15 us

profile of v1, /device:TPU:0, one launch (start us, length us, event | category | flops | bytes accessed | tf_op | source)
XLA Modules:
  0.0 102.8 jit_solution(12280194854677331808)
XLA Ops:
  0.0 0.8 reduce-window.17
  0.8 0.7 bitcast_subtract_fusion
  1.5 0.9 convert_reduce_fusion
  2.4 0.7 multiply_add_fusion
  3.1 0.1 broadcast_compare_fusion
  3.1 0.7 iota_compare_fusion.1
  3.9 0.1 lt.56
  4.0 0.1 iota_add_fusion
  4.0 0.1 add.34
  4.1 0.7 copy.16
  4.9 0.1 reduce
  5.0 0.7 sub.14
  5.7 0.1 compare_and_fusion
  5.7 0.2 and_reduce_fusion
  6.0 0.1 copy.17.member_ref
  6.1 1.8 %reshape.210.text_ref = bf16[24,8192]{1,0:T(8,128)(2,1)} reshape(bf16[6,4,8192]{2,1,0:T(4,128)(2,1)} %param.21) | data formatting | bytes 786432 | tf_op jit(solution)/shard_map/reshape | solution.py:594
  7.9 0.0 copy-start
  7.9 70.5 %vision.1 = (bf16[8,4,64,256]{3,2,1,0:T(8,128)(2,1)}, bf16[4,192,128]{2,1,0:T(8,128)(2,1)}) custom-call(bf16[256,1280]{1,0:T(8,128)(2,1)} %bitcast.9, bf16[24,8192]{1,0:T(8,128)(2,1)} %reshape.210.text_ref, bf16[1280,1280]{1,0:T(8,128)(2,1)} %fc1_hbm.1, bf16[1280,1280]{1,0:T(8,128)(2,1)} %fc2_hbm.1, bf16[1280,1024]{1,0:T(8,128)(2,1)} %key_hbm.1, ...), custom_call_target="tpu_custom_call" | custom-call | tf_op jit(solution)/shard_map/vision/pallas_call | solution.py:600
  78.4 0.0 copy-done
  78.4 0.0 copy-start.1
  78.4 1.2 %copy-done.1 = bf16[8,4,64,256]{3,2,1,0:T(8,128)(2,1)S(1)} copy-done((bf16[8,4,64,256]{3,2,1,0:T(8,128)(2,1)S(1)}, bf16[8,4,64,256]{3,2,1,0:T(8,128)(2,1)}, u32[]{:S(2)}) %copy-start.1) | copy-done | bytes 1048600
  79.6 0.0 copy-start.2
  79.6 0.9 copy-done.2
  80.5 21.6 %decode.1 = bf16[24,1024]{1,0:T(8,128)(2,1)S(1)} custom-call(bf16[4,192,128]{2,1,0:T(8,128)(2,1)S(1)} %copy-done.2, bf16[2048,256]{1,0:T(8,128)(2,1)S(1)} %bitcast.8, f32[96,64]{1,0:T(8,128)S(1)} %copy.17.member_ref, bf16[24,8192]{1,0:T(8,128)(2,1)S(1)} %copy-done, bf16[1024,8192]{1,0:T(8,128)(2,1)} %out_hbm.1), custom_call_target="tpu_custom_call" | custom-call | tf_op jit(solution)/shard_map/decode/pallas_call | solution.py:649
  102.1 0.6 reshape.216
  (3 shorter events, 0.0 us)
Async XLA Ops:
  7.9 70.5 %copy-start = (bf16[24,8192]{1,0:T(8,128)(2,1)S(1)}, bf16[24,8192]{1,0:T(8,128)(2,1)}, u32[]{:S(2)}) copy-start(bf16[24,8192]{1,0:T(8,128)(2,1)} %reshape.210.text_ref) | copy-start | bytes 1179652
  78.4 1.2 %copy-start.1 = (bf16[8,4,64,256]{3,2,1,0:T(8,128)(2,1)S(1)}, bf16[8,4,64,256]{3,2,1,0:T(8,128)(2,1)}, u32[]{:S(2)}) copy-start(bf16[8,4,64,256]{3,2,1,0:T(8,128)(2,1)} %get-tuple-element.8) | copy-start | bytes 3145732
  79.6 0.9 copy-start.2

commit v2 on v0

--- a/solution.py
+++ b/solution.py
@@ -1,7 +1,11 @@
 import jax
 import jax.numpy as jnp
 from jax import lax
+from jax.experimental import pallas as pl
+from jax.experimental.pallas import tpu as pltpu
 from jax.sharding import PartitionSpec as P
+
+MESH = pl.DeviceIdType.MESH
 
 HEADS = 64
 KV_HEADS = 8
@@ -155,9 +159,493 @@
     return mixed.reshape(slots, steps, width_out)
 
 
+def remote(source, target, send_sems, recv_sems, index, device):
+    return pltpu.make_async_remote_copy(
+        src_ref=source,
+        dst_ref=target,
+        send_sem=send_sems.at[index],
+        recv_sem=recv_sems.at[index],
+        device_id=device,
+        device_id_type=MESH,
+    )
+
+
+def greet(pool_peers, dev_peers):
+    barrier = pltpu.get_barrier_semaphore()
+    for peer in pool_peers + dev_peers:
+        pl.semaphore_signal(barrier, inc=1, device_id=peer, device_id_type=MESH)
+    pl.semaphore_wait(barrier, len(pool_peers) + len(dev_peers))
+
+
+def block_kernel(
+    enc_ref,
+    tiles_ref,
+    owner_ref,
+    patches_ref,
+    text_ref,
+    fc1_hbm,
+    fc2_hbm,
+    key_hbm,
+    value_hbm,
+    query_hbm,
+    out_hbm,
+    mixed_ref,
+    fc1,
+    fc2,
+    key_map,
+    value_map,
+    big_map,
+    rows,
+    hidden,
+    partial,
+    own_sum,
+    late_sum,
+    outbox,
+    diagonal_in,
+    x_in,
+    y_in,
+    kv_box,
+    kv_all,
+    text_raw,
+    text_normed,
+    query_sum,
+    query_flat,
+    query_all,
+    mask,
+    gathered,
+    group_out,
+    group_in,
+    attended,
+    piece_out,
+    piece_in,
+    local_sems,
+    send_sems,
+    recv_sems,
+):
+    pool, dev = lax.axis_index("pool"), lax.axis_index("dev")
+    x, y = lax.rem(pool, 2), lax.div(pool, 2)
+    x_peer = (y * 2 + 1 - x, dev)
+    y_peer = ((1 - y) * 2 + x, dev)
+    devices = kv_all.shape[1]
+    chunks = rows.shape[0]
+    part = rows.shape[1] // 4
+    width = rows.shape[2]
+    tile = 256
+    slots, steps = text_ref.shape[0], text_ref.shape[1]
+    text_rows = slots * steps
+    pieces, depth, width_out = big_map.shape
+    heads = query_sum.shape[1] // HEAD_DIM
+    pair = 2 * HEAD_DIM
+    tile_slots = 8
+
+    loads = [
+        pltpu.make_async_copy(fc1_hbm, fc1, local_sems.at[0]),
+        pltpu.make_async_copy(fc2_hbm, fc2, local_sems.at[1]),
+        pltpu.make_async_copy(key_hbm, key_map, local_sems.at[2]),
+        pltpu.make_async_copy(value_hbm, value_map, local_sems.at[3]),
+    ]
+    query_loads = [
+        pltpu.make_async_copy(
+            query_hbm.at[pl.ds(k * depth, depth), :], big_map.at[k], local_sems.at[4 + k]
+        )
+        for k in range(pieces)
+    ]
+    out_loads = [
+        pltpu.make_async_copy(
+            out_hbm.at[
+                :, pl.ds(pl.multiple_of(lax.rem(dev + k, devices) * width_out, width_out), width_out)
+            ],
+            big_map.at[k],
+            local_sems.at[4 + pieces + k],
+        )
+        for k in range(devices)
+    ]
+    for load in query_loads[:4] + loads[:2] + query_loads[4:] + loads[2:]:
+        load.start()
+
+    pool_peers = [(lax.rem(pool + k, 4), dev) for k in range(1, 4)]
+    dev_peers = [(pool, lax.rem(dev + k, devices)) for k in range(1, devices)]
+
+    def normalize(c):
+        values = patches_ref[c * part : (c + 1) * part, :].astype(jnp.float32)
+        rows[c, 0:part, :] = layer_stats(values).astype(jnp.bfloat16)
+
+    normalize(0)
+    greet(pool_peers, dev_peers)
+
+    count = [0]
+    everything = []
+
+    def send(source, target, device):
+        copy = remote(source, target, send_sems, recv_sems, count[0], device)
+        count[0] += 1
+        everything.append(copy)
+        return copy
+
+    def block(c, k):
+        return rows.at[c, pl.ds(k * part, part)]
+
+    to_x = [send(block(c, 0), block(c, 1), x_peer) for c in range(chunks)]
+    to_y = [send(block(c, 0), block(c, 2), y_peer) for c in range(chunks)]
+    onward = [
+        send(block(c, 1), block(c, 3), y_peer)
+        if c % 2 == 0
+        else send(block(c, 2), block(c, 3), x_peer)
+        for c in range(chunks)
+    ]
+
+    def forward(c):
+        first = to_x[c] if c % 2 == 0 else to_y[c]
+        first.wait_recv()
+        onward[c].start()
+
+    def arrive(c):
+        second = to_y[c] if c % 2 == 0 else to_x[c]
+        second.wait_recv()
+        onward[c].wait_recv()
+
+    to_x[0].start()
+    to_y[0].start()
+    normalize(1)
+    to_y[1].start()
+    to_x[1].start()
+
+    for s in range(slots):
+        text_raw[s * steps : (s + 1) * steps, :] = text_ref[s].astype(jnp.float32)
+    text_normed[...] = rms_scale(text_raw[...])
+    query_sum[...] = jnp.zeros_like(query_sum)
+
+    def query_step(k):
+        query_loads[k].wait()
+        query_sum[...] += jnp.dot(
+            text_normed[:, k * depth : (k + 1) * depth].astype(jnp.bfloat16),
+            big_map[k],
+            preferred_element_type=jnp.float32,
+        )
+
+    for c in range(2, chunks):
+        normalize(c)
+    query_step(0)
+    query_step(1)
+    forward(0)
+    forward(1)
+    for c in range(2, chunks):
+        to_x[c].start()
+        to_y[c].start()
+    for k in range(2, pieces):
+        query_step(k)
+    for load in out_loads[1:] + out_loads[:1]:
+        load.start()
+    for h in range(heads):
+        query_flat[h * text_rows : (h + 1) * text_rows, :] = rms_scale(
+            query_sum[:, h * HEAD_DIM : (h + 1) * HEAD_DIM]
+        )
+    query_all[pool] = query_flat[...].astype(jnp.bfloat16)
+    query_sends = [send(query_all.at[pool], query_all.at[pool], peer) for peer in pool_peers]
+    for copy in query_sends:
+        copy.start()
+
+    def tables():
+        span = devices * part
+        requests = tiles_ref.shape[0]
+        quarter = part * chunks // tile_slots
+        column = lax.broadcasted_iota(jnp.int32, (text_rows, span), 1)
+        row_slot = lax.div(lax.broadcasted_iota(jnp.int32, (text_rows, span), 0), steps)
+        source = lax.div(column, part)
+        inner = lax.div(lax.rem(column, part), quarter)
+        begin = jnp.zeros((text_rows, span), jnp.int32)
+        size = jnp.zeros((text_rows, span), jnp.int32)
+        running = 0
+        for e in range(devices):
+            begin = jnp.where(source == e, running, begin)
+            size = jnp.where(source == e, enc_ref[e], size)
+            running = running + enc_ref[e]
+        owners = [owner_ref[r, 0] for r in range(requests)]
+        names, starts, ends = [], [], []
+        running = 0
+        for r in range(requests):
+            rank = 0
+            for earlier in range(r):
+                rank = rank + jnp.where(owners[earlier] == owners[r], 1, 0)
+            names.append(owners[r] * slots + rank)
+            starts.append(running)
+            running = running + tiles_ref[r]
+            ends.append(running)
+        for c in range(chunks):
+            place = inner + c * (part // quarter)
+            index = begin + place
+            name = jnp.full((text_rows, span), -1, jnp.int32)
+            for r in range(requests):
+                name = jnp.where((index >= starts[r]) & (index < ends[r]), names[r], name)
+            name = jnp.where(place < size, name, -1)
+            for g in range(4):
+                mask[c, g] = jnp.where(row_slot + g * slots == name, 1.0, 0.0)
+
+    tables()
+    gathered[...] = jnp.zeros_like(gathered)
+
+    def feed_forward(c):
+        for n in range(fc1.shape[1] // tile):
+            columns = slice(n * tile, (n + 1) * tile)
+            pre = jnp.dot(rows[c], fc1[:, columns], preferred_element_type=jnp.float32)
+            hidden[:, columns] = (0.5 * pre * (1.0 + lax.erf(pre * 0.7071067811865476))).astype(
+                jnp.bfloat16
+            )
+        for n in range(width // tile):
+            columns = slice(n * tile, (n + 1) * tile)
+            partial[:, columns] = jnp.dot(
+                hidden[...], fc2[:, columns], preferred_element_type=jnp.float32
+            )
+        late = 2 if c % 2 == 0 else 1
+        early = 3 - late
+        outbox[c, 0] = partial[3 * part : 4 * part, :].astype(jnp.bfloat16)
+        peer = x_peer if c % 2 == 0 else y_peer
+        arrival = x_in if c % 2 == 0 else y_in
+        copies = [send(outbox.at[c, 0], diagonal_in.at[c], peer)]
+        copies[0].start()
+        outbox[c, 1] = partial[early * part : (early + 1) * part, :].astype(jnp.bfloat16)
+        copies.append(send(outbox.at[c, 1], arrival.at[c], peer))
+        copies[1].start()
+        own_sum[c] = partial[0:part, :]
+        late_sum[c] = partial[late * part : (late + 1) * part, :]
+        sums[c] = copies
+
+    def pass_on(c):
+        sums[c][0].wait_recv()
+        outbox[c, 2] = (late_sum[c] + diagonal_in[c].astype(jnp.float32)).astype(jnp.bfloat16)
+        peer = y_peer if c % 2 == 0 else x_peer
+        arrival = y_in if c % 2 == 0 else x_in
+        copy = send(outbox.at[c, 2], arrival.at[c], peer)
+        copy.start()
+        sums[c].append(copy)
+
+    def project(c):
+        sums[c][1].wait_recv()
+        sums[c][2].wait_recv()
+        if c == 0:
+            loads[2].wait()
+            loads[3].wait()
+        update = own_sum[c] + x_in[c].astype(jnp.float32) + y_in[c].astype(jnp.float32)
+        vision = (
+            patches_ref[c * part : (c + 1) * part, :].astype(jnp.float32) + update
+        ).astype(jnp.bfloat16)
+        for n in range(KV_HEADS // 2):
+            columns = slice(n * pair, (n + 1) * pair)
+            keys = jnp.dot(vision, key_map[:, columns], preferred_element_type=jnp.float32)
+            values = jnp.dot(vision, value_map[:, columns], preferred_element_type=jnp.float32)
+            for i in range(2):
+                lanes = slice(i * HEAD_DIM, (i + 1) * HEAD_DIM)
+                kv_box[c, 2 * n + i, :, 0:HEAD_DIM] = rms_scale(keys[:, lanes]).astype(jnp.bfloat16)
+                kv_box[c, 2 * n + i, :, HEAD_DIM:pair] = values[:, lanes].astype(jnp.bfloat16)
+        kv_all[c, dev] = kv_box[c, dev]
+        kv_sends[c] = [
+            send(kv_box.at[c, peer[1]], kv_all.at[c, dev], peer) for peer in dev_peers
+        ]
+        for copy in kv_sends[c]:
+            copy.start()
+
+    def attend(c, group):
+        keys = kv_all[c, :, :, 0:HEAD_DIM].reshape(devices * part, HEAD_DIM)
+        values = kv_all[c, :, :, HEAD_DIM:pair].reshape(devices * part, HEAD_DIM)
+        scores = lax.dot_general(
+            query_all[group], keys, (((1,), (1,)), ((), ())), preferred_element_type=jnp.float32
+        ) * HEAD_DIM ** (-0.5)
+        weights = (
+            jnp.exp(scores).reshape(heads, text_rows, devices * part) * mask[c, group][None]
+        )
+        gathered[group] += jnp.dot(
+            weights.reshape(heads * text_rows, devices * part).astype(jnp.bfloat16),
+            jnp.concatenate([values, jnp.ones_like(values)], axis=1),
+            preferred_element_type=jnp.float32,
+        )
+
+    def attend_all(c):
+        for copy in kv_sends[c]:
+            copy.wait_recv()
+
+        def step(g, carry):
+            attend(c, g)
+            return carry
+
+        lax.fori_loop(0, 4, step, 0)
+
+    sums = [None] * chunks
+    kv_sends = [None] * chunks
+    loads[0].wait()
+    loads[1].wait()
+    arrive(0)
+    feed_forward(0)
+    forward(2)
+    arrive(1)
+    feed_forward(1)
+    forward(3)
+    pass_on(0)
+    pass_on(1)
+    arrive(2)
+    feed_forward(2)
+    project(0)
+    arrive(3)
+    feed_forward(3)
+    pass_on(2)
+    project(1)
+    pass_on(3)
+    for copy in query_sends:
+        copy.wait_recv()
+    attend_all(0)
+    project(2)
+    project(3)
+    attend_all(1)
+    attend_all(2)
+    for copy in kv_sends[3]:
+        copy.wait_recv()
+
+    lane = lax.broadcasted_iota(jnp.int32, (heads * text_rows, HEAD_DIM), 1)
+    group_sends = []
+    for k, peer in enumerate(pool_peers):
+        group = peer[0]
+        attend(3, group)
+        total = gathered[group, :, HEAD_DIM:pair]
+        coarse = total.astype(jnp.bfloat16).astype(jnp.float32)
+        group_out[k, :, 0:HEAD_DIM] = gathered[group, :, 0:HEAD_DIM].astype(jnp.bfloat16)
+        group_out[k, :, HEAD_DIM:pair] = jnp.where(
+            lane < HEAD_DIM // 2, coarse, total - coarse
+        ).astype(jnp.bfloat16)
+        copy = send(group_out.at[k], group_in.at[k], peer)
+        copy.start()
+        group_sends.append(copy)
+    attend(3, pool)
+    top = gathered[pool, :, 0:HEAD_DIM]
+    total = gathered[pool, :, HEAD_DIM : HEAD_DIM + 1]
+    middle = HEAD_DIM + HEAD_DIM // 2
+    for k, copy in enumerate(group_sends):
+        copy.wait_recv()
+        arrived = group_in[k].astype(jnp.float32)
+        top = top + arrived[:, 0:HEAD_DIM]
+        total = total + (arrived[:, HEAD_DIM : HEAD_DIM + 1] + arrived[:, middle : middle + 1])
+    result = top / jnp.where(total > 0.0, total, 1.0)
+    for h in range(heads):
+        attended[:, h * HEAD_DIM : (h + 1) * HEAD_DIM] = result[
+            h * text_rows : (h + 1) * text_rows, :
+        ]
+    left = attended[...].astype(jnp.bfloat16)
+    half = width_out // 2
+
+    def piece(k):
+        out_loads[k].wait()
+        product = jnp.dot(left, big_map[k], preferred_element_type=jnp.float32)
+        return jnp.concatenate([product[:, :half], product[:, half:]], axis=0)
+
+    copies = []
+    for k in range(1, devices):
+        piece_out[k - 1] = piece(k).astype(jnp.bfloat16)
+        copy = send(piece_out.at[k - 1], piece_in.at[k - 1], dev_peers[k - 1])
+        copy.start()
+        copies.append(copy)
+    folded = piece(0)
+    for k, copy in enumerate(copies):
+        copy.wait_recv()
+        folded = folded + piece_in[k].astype(jnp.float32)
+    own = pl.ds(pl.multiple_of(dev * width_out, width_out), width_out)
+    summed = jnp.concatenate([folded[:text_rows], folded[text_rows:]], axis=1)
+    mixed = (text_raw[:, own] + summed).astype(jnp.bfloat16).astype(jnp.float32)
+    for s in range(slots):
+        mixed_ref[s] = mixed[s * steps : (s + 1) * steps, :].astype(jnp.bfloat16)
+    for copy in everything:
+        copy.wait_send()
+
+
+def fused_body(
+    patches,
+    enc_tiles,
+    req_tiles,
+    req_owner,
+    fc1_weight,
+    fc2_weight,
+    key_weight,
+    value_weight,
+    query_weight,
+    out_weight,
+    text_hidden,
+):
+    capacity, quarter, width = patches.shape
+    slots, steps, model_width = text_hidden.shape
+    groups, devices = lax.axis_size("pool"), lax.axis_size("dev")
+    local = query_weight.shape[1]
+    heads = local // HEAD_DIM
+    chunks = 4
+    count = capacity * quarter
+    part = count // chunks
+    text_rows = slots * steps
+    vmem = pl.BlockSpec(memory_space=pltpu.VMEM)
+    smem = pl.BlockSpec(memory_space=pltpu.SMEM)
+    anywhere = pl.BlockSpec(memory_space=pl.ANY)
+    bf16, f32 = jnp.bfloat16, jnp.float32
+    width_out = model_width // devices
+    pieces = model_width // width_out
+    copies = 6 * chunks + 2 * (groups - 1) + (chunks + 1) * (devices - 1)
+    group_box = (groups - 1, heads * text_rows, 2 * HEAD_DIM)
+    piece = (devices - 1, 2 * text_rows, width_out // 2)
+    return pl.pallas_call(
+        block_kernel,
+        out_shape=jax.ShapeDtypeStruct((slots, steps, width_out), bf16),
+        in_specs=[smem] * 3 + [vmem] * 2 + [anywhere] * 6,
+        out_specs=vmem,
+        scratch_shapes=[
+            pltpu.VMEM(fc1_weight.shape, bf16),
+            pltpu.VMEM(fc2_weight.shape, bf16),
+            pltpu.VMEM(key_weight.shape, bf16),
+            pltpu.VMEM(value_weight.shape, bf16),
+            pltpu.VMEM((pieces, local, width_out), bf16),
+            pltpu.VMEM((chunks, 4 * part, width), bf16),
+            pltpu.VMEM((4 * part, fc1_weight.shape[1]), bf16),
+            pltpu.VMEM((4 * part, width), f32),
+            pltpu.VMEM((chunks, part, width), f32),
+            pltpu.VMEM((chunks, part, width), f32),
+            pltpu.VMEM((chunks, 3, part, width), bf16),
+            pltpu.VMEM((chunks, part, width), bf16),
+            pltpu.VMEM((chunks, part, width), bf16),
+            pltpu.VMEM((chunks, part, width), bf16),
+            pltpu.VMEM((chunks, KV_HEADS, part, 2 * HEAD_DIM), bf16),
+            pltpu.VMEM((chunks, devices, part, 2 * HEAD_DIM), bf16),
+            pltpu.VMEM((text_rows, model_width), f32),
+            pltpu.VMEM((text_rows, model_width), f32),
+            pltpu.VMEM((text_rows, local), f32),
+            pltpu.VMEM((heads * text_rows, HEAD_DIM), f32),
+            pltpu.VMEM((groups, heads * text_rows, HEAD_DIM), bf16),
+            pltpu.VMEM((chunks, groups, text_rows, devices * part), f32),
+            pltpu.VMEM((groups, heads * text_rows, 2 * HEAD_DIM), f32),
+            pltpu.VMEM(group_box, bf16),
+            pltpu.VMEM(group_box, bf16),
+            pltpu.VMEM((text_rows, local), f32),
+            pltpu.VMEM(piece, bf16),
+            pltpu.VMEM(piece, bf16),
+            pltpu.SemaphoreType.DMA((4 + pieces + devices,)),
+            pltpu.SemaphoreType.DMA((copies,)),
+            pltpu.SemaphoreType.DMA((copies,)),
+        ],
+        compiler_params=pltpu.CompilerParams(
+            collective_id=0, has_side_effects=True, vmem_limit_bytes=58 * 1024 * 1024
+        ),
+        name="block",
+    )(
+        enc_tiles,
+        req_tiles,
+        req_owner,
+        patches.reshape(count, width),
+        text_hidden,
+        fc1_weight,
+        fc2_weight,
+        key_weight,
+        value_weight,
+        query_weight,
+        out_weight,
+    )
+
+
 def solution(mesh):
+    fits = mesh.shape["pool"] == 4 and mesh.shape["dev"] == KV_HEADS
     return jax.shard_map(
-        body,
+        fused_body if fits else body,
         mesh=mesh,
         in_specs=(
             P("dev", "pool", None),

time: 250 us -> 92 us (0.37)
  waiting for transfers between devices: 166 us -> 0 us
  Pallas kernels: 0 us -> 88.6 us
  matrix products: 44.1 us -> 0 us
  other arithmetic: 14.5 us -> 0 us
  between operations: 13.4 us -> 0.01 us
  starting transfers between devices: 8.23 us -> 0 us
    pallas_call x0 -> x1, Pallas kernels: none -> 88.6 us  [fused_body(): pl.pallas_call(block_kernel, out_shape=jax.ShapeDtypeStruct((slots, steps...]
    reduce_scatter x2 -> x0, waiting for transfers between devices: 86.3 us -> none  [the longest x1 58 us: body(): lax.psum_scatter(jnp.dot(widened, fc2_weight, preferred_element_type=jnp....]
    dot_general x7 -> x0, matrix products: 44.1 us -> none  [the longest x1 20.5 us: body(): jnp.dot(widened, fc2_weight, preferred_element_type=jnp.float32)]
    all_gather x1 -> x0, waiting for transfers between devices: 42.4 us -> none  [body(): lax.all_gather(normed, 'pool', axis=0, tiled=True)]
    all_to_all x2 -> x0, waiting for transfers between devices: 37.1 us -> none  [the longest x1 26.2 us: body(): lax.all_to_all(copies_out, 'dev', split_axis=0, concat_axis=0, tiled=True)]
    all_to_all x2 -> x0, starting transfers between devices: 8.15 us -> none  [the longest x1 4.59 us: body(): lax.all_to_all(copies_out, 'dev', split_axis=0, concat_axis=0, tiled=True)]
    convert_element_type x8 -> x0, other arithmetic: 5.84 us -> none  [the longest x1 2.15 us: body(): normed = layer_stats(flat_patches.astype(jnp.float32)).astype(jnp.bfloat16)]
    reduce_sum x9 -> x0, other arithmetic: 5.21 us -> none  [the longest x1 1.4 us: layer_stats(): spread = jnp.mean(center * center, axis=-1, keepdims=True)]
  transfers between devices with their start and end apart: 5 -> 0, of which waited for: 5 -> 0; matrix products, arithmetic and copies ran while one was open for 5% -> 0% of each run, Pallas kernels for 0% -> 0%
where the time goes in v2:
time: 92 us; the launch traced here: 91.3 us
  Pallas kernels  88.6 us (96%)
  local copies, waits for them, and re-layouts  2.77 us (3%)
    pallas_call x1, Pallas kernels, fused_body(): pl.pallas_call(block_kernel, out_shape=jax.ShapeDtypeStruct((slots, steps...  88.6 us
    unnamed x2, local copies, waits for them, and re-layouts  2.77 us

profile of v2, /device:TPU:0, one launch (start us, length us, event | category | flops | bytes accessed | tf_op | source)
XLA Modules:
  0.0 91.3 jit_solution(13944446191218880944)
XLA Ops:
  0.0 1.3 %copy.12.owner_ref = s32[16,1]{1,0:T(8,128)} copy(s32[16,1]{0,1:T(1,128)} %param.14) | data formatting | bytes 128 | tf_op args[3]
  1.3 88.6 %block.1 = bf16[6,4,1024]{2,1,0:T(4,128)(2,1)} custom-call(s32[8]{0:T(128)} %enc_ref.1, s32[16]{0:T(128)} %tiles_ref.1, s32[16,1]{1,0:T(8,128)} %copy.12.owner_ref, bf16[256,1280]{1,0:T(8,128)(2,1)} %bitcast.1, bf16[6,4,8192]{2,1,0:T(4,128)(2,1)} %text_ref.1, bf16[1280,1280]{1,0:T(8,128)(2,1)} %fc1_hbm.1, bf16[1280,1280]{1,0:T(8,128)(2,1)} %fc2_hbm.1, ...), custom_call_target="tpu_custom_call" | custom-call | tf_op jit(solution)/shard_map/block/pallas_call | solution.py:588
  89.9 1.4 %copy.14 = bf16[6,4,1024]{2,1,0:T(4,128)(2,1)} copy(bf16[6,4,1024]{2,1,0:T(4,128)(2,1)} %block.1) | data formatting | bytes 98304

commit v3 on v2

--- a/solution.py
+++ b/solution.py
@@ -159,6 +159,17 @@
     return mixed.reshape(slots, steps, width_out)
 
 
+def center_rows(values_in):
+    center = values_in - jnp.mean(values_in, axis=-1, keepdims=True)
+    return center * lax.rsqrt(jnp.mean(center * center, axis=-1, keepdims=True) + epsilon)
+
+
+def root_rows(values_in):
+    return values_in * lax.rsqrt(
+        jnp.mean(values_in * values_in, axis=-1, keepdims=True) + epsilon
+    )
+
+
 def remote(source, target, send_sems, recv_sems, index, device):
     return pltpu.make_async_remote_copy(
         src_ref=source,
@@ -197,7 +208,6 @@
     big_map,
     rows,
     hidden,
-    partial,
     own_sum,
     late_sum,
     outbox,
@@ -268,7 +278,7 @@
 
     def normalize(c):
         values = patches_ref[c * part : (c + 1) * part, :].astype(jnp.float32)
-        rows[c, 0:part, :] = layer_stats(values).astype(jnp.bfloat16)
+        rows[c, 0:part, :] = center_rows(values).astype(jnp.bfloat16)
 
     normalize(0)
     greet(pool_peers, dev_peers)
@@ -312,7 +322,7 @@
 
     for s in range(slots):
         text_raw[s * steps : (s + 1) * steps, :] = text_ref[s].astype(jnp.float32)
-    text_normed[...] = rms_scale(text_raw[...])
+    text_normed[...] = root_rows(text_raw[...])
     query_sum[...] = jnp.zeros_like(query_sum)
 
     def query_step(k):
@@ -337,7 +347,7 @@
     for load in out_loads[1:] + out_loads[:1]:
         load.start()
     for h in range(heads):
-        query_flat[h * text_rows : (h + 1) * text_rows, :] = rms_scale(
+        query_flat[h * text_rows : (h + 1) * text_rows, :] = root_rows(
             query_sum[:, h * HEAD_DIM : (h + 1) * HEAD_DIM]
         )
     query_all[pool] = query_flat[...].astype(jnp.bfloat16)
@@ -360,7 +370,7 @@
             begin = jnp.where(source == e, running, begin)
             size = jnp.where(source == e, enc_ref[e], size)
             running = running + enc_ref[e]
-        owners = [owner_ref[r, 0] for r in range(requests)]
+        owners = [owner_ref[r] for r in range(requests)]
         names, starts, ends = [], [], []
         running = 0
         for r in range(requests):
@@ -382,7 +392,6 @@
                 mask[c, g] = jnp.where(row_slot + g * slots == name, 1.0, 0.0)
 
     tables()
-    gathered[...] = jnp.zeros_like(gathered)
 
     def feed_forward(c):
         for n in range(fc1.shape[1] // tile):
@@ -391,23 +400,25 @@
             hidden[:, columns] = (0.5 * pre * (1.0 + lax.erf(pre * 0.7071067811865476))).astype(
                 jnp.bfloat16
             )
+        late = 2 if c % 2 == 0 else 1
+        early = 3 - late
         for n in range(width // tile):
             columns = slice(n * tile, (n + 1) * tile)
-            partial[:, columns] = jnp.dot(
-                hidden[...], fc2[:, columns], preferred_element_type=jnp.float32
+            product = jnp.dot(hidden[...], fc2[:, columns], preferred_element_type=jnp.float32)
+            outbox[c, 0, :, columns] = product[3 * part : 4 * part, :].astype(jnp.bfloat16)
+            outbox[c, 1, :, columns] = product[early * part : (early + 1) * part, :].astype(
+                jnp.bfloat16
             )
-        late = 2 if c % 2 == 0 else 1
-        early = 3 - late
-        outbox[c, 0] = partial[3 * part : 4 * part, :].astype(jnp.bfloat16)
+            own_sum[c, :, columns] = product[0:part, :]
+            late_sum[c, :, columns] = product[late * part : (late + 1) * part, :]
         peer = x_peer if c % 2 == 0 else y_peer
         arrival = x_in if c % 2 == 0 else y_in
-        copies = [send(outbox.at[c, 0], diagonal_in.at[c], peer)]
-        copies[0].start()
-        outbox[c, 1] = partial[early * part : (early + 1) * part, :].astype(jnp.bfloat16)
-        copies.append(send(outbox.at[c, 1], arrival.at[c], peer))
-        copies[1].start()
-        own_sum[c] = partial[0:part, :]
-        late_sum[c] = partial[late * part : (late + 1) * part, :]
+        copies = [
+            send(outbox.at[c, 0], diagonal_in.at[c], peer),
+            send(outbox.at[c, 1], arrival.at[c], peer),
+        ]
+        for copy in copies:
+            copy.start()
         sums[c] = copies
 
     def pass_on(c):
@@ -419,55 +430,56 @@
         copy.start()
         sums[c].append(copy)
 
-    def project(c):
-        sums[c][1].wait_recv()
-        sums[c][2].wait_recv()
-        if c == 0:
+    def project(*together):
+        halves = []
+        for c in together:
+            sums[c][1].wait_recv()
+            sums[c][2].wait_recv()
+            update = own_sum[c] + x_in[c].astype(jnp.float32) + y_in[c].astype(jnp.float32)
+            halves.append(patches_ref[c * part : (c + 1) * part, :].astype(jnp.float32) + update)
+        if together[0] == 0:
             loads[2].wait()
             loads[3].wait()
-        update = own_sum[c] + x_in[c].astype(jnp.float32) + y_in[c].astype(jnp.float32)
-        vision = (
-            patches_ref[c * part : (c + 1) * part, :].astype(jnp.float32) + update
-        ).astype(jnp.bfloat16)
+        vision = jnp.concatenate(halves, axis=0).astype(jnp.bfloat16)
         for n in range(KV_HEADS // 2):
             columns = slice(n * pair, (n + 1) * pair)
             keys = jnp.dot(vision, key_map[:, columns], preferred_element_type=jnp.float32)
             values = jnp.dot(vision, value_map[:, columns], preferred_element_type=jnp.float32)
             for i in range(2):
                 lanes = slice(i * HEAD_DIM, (i + 1) * HEAD_DIM)
-                kv_box[c, 2 * n + i, :, 0:HEAD_DIM] = rms_scale(keys[:, lanes]).astype(jnp.bfloat16)
-                kv_box[c, 2 * n + i, :, HEAD_DIM:pair] = values[:, lanes].astype(jnp.bfloat16)
-        kv_all[c, dev] = kv_box[c, dev]
-        kv_sends[c] = [
-            send(kv_box.at[c, peer[1]], kv_all.at[c, dev], peer) for peer in dev_peers
-        ]
+                head_keys = root_rows(keys[:, lanes]).astype(jnp.bfloat16)
+                head_values = values[:, lanes].astype(jnp.bfloat16)
+                for t, c in enumerate(together):
+                    span = slice(t * part, (t + 1) * part)
+                    kv_box[c, 2 * n + i, :, 0:HEAD_DIM] = head_keys[span]
+                    kv_box[c, 2 * n + i, :, HEAD_DIM:pair] = head_values[span]
+        for c in together:
+            kv_sends[c] = [
+                send(kv_box.at[c, peer[1]], kv_all.at[c, dev], peer) for peer in dev_peers
+            ]
+            for copy in kv_sends[c]:
+                copy.start()
+            kv_all[c, dev] = kv_box[c, dev]
+
+    def attend(c):
         for copy in kv_sends[c]:
-            copy.start()
-
-    def attend(c, group):
+            copy.wait_recv()
         keys = kv_all[c, :, :, 0:HEAD_DIM].reshape(devices * part, HEAD_DIM)
         values = kv_all[c, :, :, HEAD_DIM:pair].reshape(devices * part, HEAD_DIM)
-        scores = lax.dot_general(
-            query_all[group], keys, (((1,), (1,)), ((), ())), preferred_element_type=jnp.float32
-        ) * HEAD_DIM ** (-0.5)
-        weights = (
-            jnp.exp(scores).reshape(heads, text_rows, devices * part) * mask[c, group][None]
-        )
-        gathered[group] += jnp.dot(
-            weights.reshape(heads * text_rows, devices * part).astype(jnp.bfloat16),
-            jnp.concatenate([values, jnp.ones_like(values)], axis=1),
-            preferred_element_type=jnp.float32,
-        )
-
-    def attend_all(c):
-        for copy in kv_sends[c]:
-            copy.wait_recv()
-
-        def step(g, carry):
-            attend(c, g)
-            return carry
-
-        lax.fori_loop(0, 4, step, 0)
+        values = jnp.concatenate([values, jnp.ones_like(values)], axis=1)
+        for g in range(4):
+            scores = lax.dot_general(
+                query_all[g], keys, (((1,), (1,)), ((), ())), preferred_element_type=jnp.float32
+            )
+            weights = jnp.exp2(scores * (HEAD_DIM ** (-0.5) * 1.4426950408889634)).reshape(
+                heads, text_rows, devices * part
+            ) * mask[c, g][None]
+            added = jnp.dot(
+                weights.reshape(heads * text_rows, devices * part).astype(jnp.bfloat16),
+                values,
+                preferred_element_type=jnp.float32,
+            )
+            gathered[g] = added if c == 0 else gathered[g] + added
 
     sums = [None] * chunks
     kv_sends = [None] * chunks
@@ -483,27 +495,24 @@
     pass_on(1)
     arrive(2)
     feed_forward(2)
-    project(0)
     arrive(3)
     feed_forward(3)
     pass_on(2)
-    project(1)
+    project(0, 1)
     pass_on(3)
+    project(2)
     for copy in query_sends:
         copy.wait_recv()
-    attend_all(0)
-    project(2)
+    attend(0)
     project(3)
-    attend_all(1)
-    attend_all(2)
-    for copy in kv_sends[3]:
-        copy.wait_recv()
+    attend(1)
+    attend(2)
+    attend(3)
 
     lane = lax.broadcasted_iota(jnp.int32, (heads * text_rows, HEAD_DIM), 1)
     group_sends = []
     for k, peer in enumerate(pool_peers):
         group = peer[0]
-        attend(3, group)
         total = gathered[group, :, HEAD_DIM:pair]
         coarse = total.astype(jnp.bfloat16).astype(jnp.float32)
         group_out[k, :, 0:HEAD_DIM] = gathered[group, :, 0:HEAD_DIM].astype(jnp.bfloat16)
@@ -513,7 +522,6 @@
         copy = send(group_out.at[k], group_in.at[k], peer)
         copy.start()
         group_sends.append(copy)
-    attend(3, pool)
     top = gathered[pool, :, 0:HEAD_DIM]
     total = gathered[pool, :, HEAD_DIM : HEAD_DIM + 1]
     middle = HEAD_DIM + HEAD_DIM // 2
@@ -547,9 +555,7 @@
         folded = folded + piece_in[k].astype(jnp.float32)
     own = pl.ds(pl.multiple_of(dev * width_out, width_out), width_out)
     summed = jnp.concatenate([folded[:text_rows], folded[text_rows:]], axis=1)
-    mixed = (text_raw[:, own] + summed).astype(jnp.bfloat16).astype(jnp.float32)
-    for s in range(slots):
-        mixed_ref[s] = mixed[s * steps : (s + 1) * steps, :].astype(jnp.bfloat16)
+    mixed_ref[...] = (text_raw[:, own] + summed).astype(jnp.bfloat16)
     for copy in everything:
         copy.wait_send()
 
@@ -585,9 +591,9 @@
     copies = 6 * chunks + 2 * (groups - 1) + (chunks + 1) * (devices - 1)
     group_box = (groups - 1, heads * text_rows, 2 * HEAD_DIM)
     piece = (devices - 1, 2 * text_rows, width_out // 2)
-    return pl.pallas_call(
+    mixed = pl.pallas_call(
         block_kernel,
-        out_shape=jax.ShapeDtypeStruct((slots, steps, width_out), bf16),
+        out_shape=jax.ShapeDtypeStruct((text_rows, width_out), bf16),
         in_specs=[smem] * 3 + [vmem] * 2 + [anywhere] * 6,
         out_specs=vmem,
         scratch_shapes=[
@@ -598,7 +604,6 @@
             pltpu.VMEM((pieces, local, width_out), bf16),
             pltpu.VMEM((chunks, 4 * part, width), bf16),
             pltpu.VMEM((4 * part, fc1_weight.shape[1]), bf16),
-            pltpu.VMEM((4 * part, width), f32),
             pltpu.VMEM((chunks, part, width), f32),
             pltpu.VMEM((chunks, part, width), f32),
             pltpu.VMEM((chunks, 3, part, width), bf16),
@@ -630,7 +635,7 @@
     )(
         enc_tiles,
         req_tiles,
-        req_owner,
+        req_owner.reshape(-1),
         patches.reshape(count, width),
         text_hidden,
         fc1_weight,
@@ -640,6 +645,7 @@
         query_weight,
         out_weight,
     )
+    return mixed.reshape(slots, steps, width_out)
 
 
 def solution(mesh):

time: 92 us -> 91.5 us (level)
  local copies, waits for them, and re-layouts: 2.77 us -> 1.44 us
    unnamed x2 -> x0, local copies, waits for them, and re-layouts: 2.77 us -> none
    reshape x0 -> x1, local copies, waits for them, and re-layouts: none -> 1.44 us  [fused_body(): return mixed.reshape(slots, steps, width_out)]
where the time goes in v3:
time: 91.5 us; the launch traced here: 90.9 us
  Pallas kernels  89.5 us (98%)
  local copies, waits for them, and re-layouts  1.44 us (2%)
    pallas_call x1, Pallas kernels, fused_body(): pl.pallas_call(block_kernel, out_shape=jax.ShapeDtypeStruct((text_rows, w...  89.5 us

profile of v3, /device:TPU:0, one launch (start us, length us, event | category | flops | bytes accessed | tf_op | source)
XLA Modules:
  0.0 90.9 jit_solution(11002417237696847599)
XLA Ops:
  0.0 89.5 %block.1 = bf16[24,1024]{1,0:T(8,128)(2,1)} custom-call(s32[8]{0:T(128)} %enc_ref.1, s32[16]{0:T(128)} %tiles_ref.1, s32[16]{0:T(128)} %bitcast.3, bf16[256,1280]{1,0:T(8,128)(2,1)} %bitcast.2, bf16[6,4,8192]{2,1,0:T(4,128)(2,1)} %text_ref.1, bf16[1280,1280]{1,0:T(8,128)(2,1)} %fc1_hbm.1, bf16[1280,1280]{1,0:T(8,128)(2,1)} %fc2_hbm.1, ...), custom_call_target="tpu_custom_call" | custom-call | tf_op jit(solution)/shard_map/block/pallas_call | solution.py:594
  89.5 1.4 %reshape.11 = bf16[6,4,1024]{2,1,0:T(4,128)(2,1)} reshape(bf16[24,1024]{1,0:T(8,128)(2,1)} %block.1) | data formatting | bytes 98304 | tf_op jit(solution)/shard_map/reshape | solution.py:648

commit v4 on v3

--- a/solution.py
+++ b/solution.py
@@ -225,7 +225,11 @@
     gathered,
     group_out,
     group_in,
+    total_out,
+    total_in,
     attended,
+    pair_out,
+    pair_in,
     piece_out,
     piece_in,
     local_sems,
@@ -260,15 +264,18 @@
         )
         for k in range(pieces)
     ]
+    chips = devices // 2
+    chip, core = lax.div(dev, 2), lax.rem(dev, 2)
+    ahead = [lax.rem(chip + k, chips) for k in list(range(1, chips)) + [0]]
+    targets = [place * 2 + 1 - core for place in ahead] + [place * 2 + core for place in ahead]
+    partner = (pool, chip * 2 + 1 - core)
     out_loads = [
         pltpu.make_async_copy(
-            out_hbm.at[
-                :, pl.ds(pl.multiple_of(lax.rem(dev + k, devices) * width_out, width_out), width_out)
-            ],
+            out_hbm.at[:, pl.ds(pl.multiple_of(target * width_out, width_out), width_out)],
             big_map.at[k],
             local_sems.at[4 + pieces + k],
         )
-        for k in range(devices)
+        for k, target in enumerate(targets)
     ]
     for load in query_loads[:4] + loads[:2] + query_loads[4:] + loads[2:]:
         load.start()
@@ -344,7 +351,7 @@
         to_y[c].start()
     for k in range(2, pieces):
         query_step(k)
-    for load in out_loads[1:] + out_loads[:1]:
+    for load in out_loads:
         load.start()
     for h in range(heads):
         query_flat[h * text_rows : (h + 1) * text_rows, :] = root_rows(
@@ -495,10 +502,11 @@
     pass_on(1)
     arrive(2)
     feed_forward(2)
+    project(0)
     arrive(3)
     feed_forward(3)
     pass_on(2)
-    project(0, 1)
+    project(1)
     pass_on(3)
     project(2)
     for copy in query_sends:
@@ -509,27 +517,41 @@
     attend(2)
     attend(3)
 
-    lane = lax.broadcasted_iota(jnp.int32, (heads * text_rows, HEAD_DIM), 1)
+    row = lax.broadcasted_iota(jnp.int32, (16, pair), 0)
+    lane = lax.broadcasted_iota(jnp.int32, (16, pair), 1)
+    pick = jnp.where((lane == row * HEAD_DIM) & (row < 2), 1.0, 0.0).astype(jnp.bfloat16)
     group_sends = []
     for k, peer in enumerate(pool_peers):
         group = peer[0]
-        total = gathered[group, :, HEAD_DIM:pair]
-        coarse = total.astype(jnp.bfloat16).astype(jnp.float32)
-        group_out[k, :, 0:HEAD_DIM] = gathered[group, :, 0:HEAD_DIM].astype(jnp.bfloat16)
-        group_out[k, :, HEAD_DIM:pair] = jnp.where(
-            lane < HEAD_DIM // 2, coarse, total - coarse
-        ).astype(jnp.bfloat16)
+        group_out[k] = gathered[group, :, 0:HEAD_DIM].astype(jnp.bfloat16)
         copy = send(group_out.at[k], group_in.at[k], peer)
         copy.start()
         group_sends.append(copy)
+    for k, peer in enumerate(pool_peers):
+        total = gathered[peer[0], :, HEAD_DIM:pair]
+        coarse = total.astype(jnp.bfloat16)
+        fine = (total - coarse.astype(jnp.float32)).astype(jnp.bfloat16)
+        total_out[k] = lax.dot_general(
+            pick,
+            jnp.concatenate([coarse, fine], axis=1),
+            (((1,), (1,)), ((), ())),
+            preferred_element_type=jnp.float32,
+        ).astype(jnp.bfloat16)
+        copy = send(total_out.at[k], total_in.at[k], peer)
+        copy.start()
+        group_sends.append(copy)
+    for copy in group_sends:
+        copy.wait_recv()
     top = gathered[pool, :, 0:HEAD_DIM]
-    total = gathered[pool, :, HEAD_DIM : HEAD_DIM + 1]
-    middle = HEAD_DIM + HEAD_DIM // 2
-    for k, copy in enumerate(group_sends):
-        copy.wait_recv()
-        arrived = group_in[k].astype(jnp.float32)
-        top = top + arrived[:, 0:HEAD_DIM]
-        total = total + (arrived[:, HEAD_DIM : HEAD_DIM + 1] + arrived[:, middle : middle + 1])
+    for k in range(3):
+        top = top + group_in[k].astype(jnp.float32)
+    totals = jnp.concatenate([total_in[k] for k in range(3)], axis=0)
+    total = gathered[pool, :, HEAD_DIM:pair] + lax.dot_general(
+        totals,
+        jnp.ones((totals.shape[0], HEAD_DIM), jnp.bfloat16),
+        (((0,), (0,)), ((), ())),
+        preferred_element_type=jnp.float32,
+    )
     result = top / jnp.where(total > 0.0, total, 1.0)
     for h in range(heads):
         attended[:, h * HEAD_DIM : (h + 1) * HEAD_DIM] = result[
@@ -543,13 +565,22 @@
         product = jnp.dot(left, big_map[k], preferred_element_type=jnp.float32)
         return jnp.concatenate([product[:, :half], product[:, half:]], axis=0)
 
+    handed = []
+    for k in range(chips):
+        pair_out[k] = piece(k).astype(jnp.bfloat16)
+        copy = send(pair_out.at[k], pair_in.at[k], partner)
+        copy.start()
+        handed.append(copy)
     copies = []
-    for k in range(1, devices):
-        piece_out[k - 1] = piece(k).astype(jnp.bfloat16)
-        copy = send(piece_out.at[k - 1], piece_in.at[k - 1], dev_peers[k - 1])
-        copy.start()
-        copies.append(copy)
-    folded = piece(0)
+    for k in range(chips):
+        folded = piece(chips + k)
+        handed[k].wait_recv()
+        folded = folded + pair_in[k].astype(jnp.float32)
+        if k < chips - 1:
+            piece_out[k] = folded.astype(jnp.bfloat16)
+            copy = send(piece_out.at[k], piece_in.at[k], (pool, targets[chips + k]))
+            copy.start()
+            copies.append(copy)
     for k, copy in enumerate(copies):
         copy.wait_recv()
         folded = folded + piece_in[k].astype(jnp.float32)
@@ -588,9 +619,10 @@
     bf16, f32 = jnp.bfloat16, jnp.float32
     width_out = model_width // devices
     pieces = model_width // width_out
-    copies = 6 * chunks + 2 * (groups - 1) + (chunks + 1) * (devices - 1)
-    group_box = (groups - 1, heads * text_rows, 2 * HEAD_DIM)
-    piece = (devices - 1, 2 * text_rows, width_out // 2)
+    copies = 6 * chunks + 3 * (groups - 1) + (chunks + 1) * (devices - 1)
+    group_box = (groups - 1, heads * text_rows, HEAD_DIM)
+    total_box = (groups - 1, 16, heads * text_rows)
+    piece = (2 * text_rows, width_out // 2)
     mixed = pl.pallas_call(
         block_kernel,
         out_shape=jax.ShapeDtypeStruct((text_rows, width_out), bf16),
@@ -621,9 +653,13 @@
             pltpu.VMEM((groups, heads * text_rows, 2 * HEAD_DIM), f32),
             pltpu.VMEM(group_box, bf16),
             pltpu.VMEM(group_box, bf16),
+            pltpu.VMEM(total_box, bf16),
+            pltpu.VMEM(total_box, bf16),
             pltpu.VMEM((text_rows, local), f32),
-            pltpu.VMEM(piece, bf16),
-            pltpu.VMEM(piece, bf16),
+            pltpu.VMEM((devices // 2,) + piece, bf16),
+            pltpu.VMEM((devices // 2,) + piece, bf16),
+            pltpu.VMEM((devices // 2 - 1,) + piece, bf16),
+            pltpu.VMEM((devices // 2 - 1,) + piece, bf16),
             pltpu.SemaphoreType.DMA((4 + pieces + devices,)),
             pltpu.SemaphoreType.DMA((copies,)),
             pltpu.SemaphoreType.DMA((copies,)),

time: 91.5 us -> 87.8 us (0.960)
  Pallas kernels: 89.5 us -> 86.1 us
    pallas_call x1, Pallas kernels: 89.5 us -> 86.1 us  [fused_body(): pl.pallas_call(block_kernel, out_shape=jax.ShapeDtypeStruct((text_rows, w...]
where the time goes in v4:
time: 87.8 us; the launch traced here: 87.6 us
  Pallas kernels  86.1 us (98%)
  local copies, waits for them, and re-layouts  1.44 us (2%)
    pallas_call x1, Pallas kernels, fused_body(): pl.pallas_call(block_kernel, out_shape=jax.ShapeDtypeStruct((text_rows, w...  86.1 us

profile of v4, /device:TPU:0, one launch (start us, length us, event | category | flops | bytes accessed | tf_op | source)
XLA Modules:
  0.0 87.6 jit_solution(16468546646816195876)
XLA Ops:
  0.0 86.1 %block.1 = bf16[24,1024]{1,0:T(8,128)(2,1)} custom-call(s32[8]{0:T(128)} %enc_ref.1, s32[16]{0:T(128)} %tiles_ref.1, s32[16]{0:T(128)} %bitcast.3, bf16[256,1280]{1,0:T(8,128)(2,1)} %bitcast.2, bf16[6,4,8192]{2,1,0:T(4,128)(2,1)} %text_ref.1, bf16[1280,1280]{1,0:T(8,128)(2,1)} %fc1_hbm.1, bf16[1280,1280]{1,0:T(8,128)(2,1)} %fc2_hbm.1, ...), custom_call_target="tpu_custom_call" | custom-call | tf_op jit(solution)/shard_map/block/pallas_call | solution.py:626
  86.1 1.4 %reshape.11 = bf16[6,4,1024]{2,1,0:T(4,128)(2,1)} reshape(bf16[24,1024]{1,0:T(8,128)(2,1)} %block.1) | data formatting | bytes 98304 | tf_op jit(solution)/shard_map/reshape | solution.py:684

commit v5 on v4

--- a/solution.py
+++ b/solution.py
@@ -277,7 +277,7 @@
         )
         for k, target in enumerate(targets)
     ]
-    for load in query_loads[:4] + loads[:2] + query_loads[4:] + loads[2:]:
+    for load in query_loads[:3] + loads[:2] + query_loads[3:] + loads[2:]:
         load.start()
 
     pool_peers = [(lax.rem(pool + k, 4), dev) for k in range(1, 4)]
@@ -349,18 +349,22 @@
     for c in range(2, chunks):
         to_x[c].start()
         to_y[c].start()
-    for k in range(2, pieces):
-        query_step(k)
-    for load in out_loads:
-        load.start()
-    for h in range(heads):
-        query_flat[h * text_rows : (h + 1) * text_rows, :] = root_rows(
-            query_sum[:, h * HEAD_DIM : (h + 1) * HEAD_DIM]
-        )
-    query_all[pool] = query_flat[...].astype(jnp.bfloat16)
-    query_sends = [send(query_all.at[pool], query_all.at[pool], peer) for peer in pool_peers]
-    for copy in query_sends:
-        copy.start()
+    query_step(2)
+
+    def finish_query():
+        for load in out_loads:
+            load.start()
+        for h in range(heads):
+            query_flat[h * text_rows : (h + 1) * text_rows, :] = root_rows(
+                query_sum[:, h * HEAD_DIM : (h + 1) * HEAD_DIM]
+            )
+        query_all[pool] = query_flat[...].astype(jnp.bfloat16)
+        for peer in pool_peers:
+            copy = send(query_all.at[pool], query_all.at[pool], peer)
+            copy.start()
+            query_sends.append(copy)
+
+    query_sends = []
 
     def tables():
         span = devices * part
@@ -398,7 +402,6 @@
             for g in range(4):
                 mask[c, g] = jnp.where(row_slot + g * slots == name, 1.0, 0.0)
 
-    tables()
 
     def feed_forward(c):
         for n in range(fc1.shape[1] // tile):
@@ -500,6 +503,8 @@
     forward(3)
     pass_on(0)
     pass_on(1)
+    for k in range(3, 6):
+        query_step(k)
     arrive(2)
     feed_forward(2)
     project(0)
@@ -508,7 +513,11 @@
     pass_on(2)
     project(1)
     pass_on(3)
+    for k in range(6, pieces):
+        query_step(k)
+    finish_query()
     project(2)
+    tables()
     for copy in query_sends:
         copy.wait_recv()
     attend(0)

time: 87.8 us -> 85.5 us (0.974)
  Pallas kernels: 86.1 us -> 83.9 us
    pallas_call x1, Pallas kernels: 86.1 us -> 83.9 us  [fused_body(): pl.pallas_call(block_kernel, out_shape=jax.ShapeDtypeStruct((text_rows, w...]
where the time goes in v5:
time: 85.5 us; the launch traced here: 85.4 us
  Pallas kernels  83.9 us (98%)
  local copies, waits for them, and re-layouts  1.44 us (2%)
    pallas_call x1, Pallas kernels, fused_body(): pl.pallas_call(block_kernel, out_shape=jax.ShapeDtypeStruct((text_rows, w...  83.9 us

profile of v5, /device:TPU:0, one launch (start us, length us, event | category | flops | bytes accessed | tf_op | source)
XLA Modules:
  0.0 85.4 jit_solution(8979176548131842149)
XLA Ops:
  0.0 83.9 %block.1 = bf16[24,1024]{1,0:T(8,128)(2,1)} custom-call(s32[8]{0:T(128)} %enc_ref.1, s32[16]{0:T(128)} %tiles_ref.1, s32[16]{0:T(128)} %bitcast.3, bf16[256,1280]{1,0:T(8,128)(2,1)} %bitcast.2, bf16[6,4,8192]{2,1,0:T(4,128)(2,1)} %text_ref.1, bf16[1280,1280]{1,0:T(8,128)(2,1)} %fc1_hbm.1, bf16[1280,1280]{1,0:T(8,128)(2,1)} %fc2_hbm.1, ...), custom_call_target="tpu_custom_call" | custom-call | tf_op jit(solution)/shard_map/block/pallas_call | solution.py:635
  83.9 1.4 %reshape.11 = bf16[6,4,1024]{2,1,0:T(4,128)(2,1)} reshape(bf16[24,1024]{1,0:T(8,128)(2,1)} %block.1) | data formatting | bytes 98304 | tf_op jit(solution)/shard_map/reshape | solution.py:693
